TPU v7x, 256 devices: a whole 4x4x8 slice. The times are simulated.
256 devices in a mesh: dp: 4 (over x_lo, core), fsdp: 64 (over z, y, x_hi).
Axes of the slice: x: 4 (x_hi: 2, x_lo: 2; x = x_hi * 2 + x_lo), y: 4, z: 8, core: 2. Of those that a mesh axis runs over, the one named last changes fastest.
Arguments:
- train_hidden: bfloat16 [65536, 5120], P('fsdp'), may hold values from -6 to 6
- index_hidden: bfloat16 [4096, 5120], P('dp', 'fsdp'), may hold values from -6 to 6
- index_resid: bfloat16 [4096, 2048], P('fsdp', 'dp'), may hold values from -6 to 6
- basis: float32 [8, 5120, 2048], P(None, 'fsdp', 'dp'), may hold values from -6 to 6
Outputs:
- new_basis: float32 [1, 5120, 2048], P(None, 'fsdp', 'dp')
- hessenberg: float32 [1, 9], replicated
- projections: float32 [128, 9], P('dp')
All inputs are finite; a program needn't handle non-finite values.
Results may differ from a plain program's by a relative error of at most 0.011.
Values may be sent and summed in bfloat16 or wider, within the bound.
A program may use at most 128 MiB of HBM per device.

v0:
```python
import jax
import jax.numpy as jnp
from jax import lax
from jax.sharding import PartitionSpec as P

D = 2048
FF = 5120
EX_TOK = 32
K = 8
ITERS = 1


def local(train_hidden, index_hidden, index_resid, basis):
    mean_scale = 1.0 / (FF * D)
    token_total = train_hidden.shape[0] * lax.axis_size("fsdp")
    vectors = [basis[position] for position in range(K)]
    direction = basis[K - 1]
    narrow = direction.astype(jnp.bfloat16)
    columns = train_hidden
    image = jnp.dot(
        columns,
        lax.all_gather(narrow, "fsdp", axis=0, tiled=True),
        preferred_element_type=jnp.float32,
    ).astype(jnp.bfloat16)
    columns = train_hidden
    curved = (
        lax.psum_scatter(
            lax.dot_general(
                columns, image, (((0,), (0,)), ((), ())), preferred_element_type=jnp.float32
            ),
            "fsdp",
            scatter_dimension=0,
            tiled=True,
        )
        / token_total
    )
    stacked = jnp.stack(vectors)
    local_products = jnp.sum(stacked * curved[None], axis=(1, 2))
    coeffs = lax.psum(local_products, ("dp", "fsdp")) * mean_scale
    orth = curved - jnp.sum(coeffs[:, None, None] * stacked, axis=0)
    beta = jnp.sqrt(lax.psum(jnp.sum(orth * orth), ("dp", "fsdp")) * mean_scale)
    direction = orth / beta
    padding = jnp.zeros((K + ITERS - len(vectors) - 1,), jnp.float32)
    columns_out = [jnp.concatenate([coeffs, beta[None], padding])]
    vectors.append(direction)
    fresh = [direction]
    every_hidden = lax.all_gather(index_hidden, "dp", axis=0, tiled=True)
    every_resid = lax.all_gather(index_resid, "fsdp", axis=0, tiled=True)
    narrow_basis = jnp.stack(vectors).astype(jnp.bfloat16)
    mapped = jnp.einsum(
        "td,nfd->ntf", every_resid, narrow_basis, preferred_element_type=jnp.float32
    )
    per_token = jnp.sum(mapped * every_hidden.astype(jnp.float32)[None], axis=2)
    example_count = per_token.shape[1] // EX_TOK
    partial_value = jnp.sum(
        per_token.reshape(per_token.shape[0], example_count, EX_TOK), axis=2
    ).T * (FF * D) ** (-0.5)
    owned = example_count // lax.axis_size("dp")
    totals = lax.psum(partial_value, ("dp", "fsdp"))
    projections = lax.dynamic_slice_in_dim(totals, lax.axis_index("dp") * owned, owned, 0)
    return (jnp.stack(fresh), jnp.stack(columns_out), projections)


def solution(mesh):
    in_specs = (P("fsdp", None), P("dp", "fsdp"), P("fsdp", "dp"), P(None, "fsdp", "dp"))
    out_specs = (P(None, "fsdp", "dp"), P(), P("dp", None))
    return jax.shard_map(local, mesh=mesh, in_specs=in_specs, out_specs=out_specs, check_vma=False)
```

profile of v0, /device:TPU:1, one launch (start us, length us, event | category | flops | bytes accessed | tf_op | source)
XLA Modules:
  0.0 829.8 jit_solution(13876991454773166997)
XLA Ops:
  7.2 0.0 all-gather.6.cloned.1.call-start
  7.2 1.4 convert.7
  8.6 0.6 slice.6
  9.3 0.0 all-gather.6.cloned.1.call-update
  9.3 0.0 reduce-scatter.4.cloned.1.call-start
  9.3 137.0 %all-gather.6.cloned.1.call-done = bf16[1,5120,512]{2,1,0:T(8,128)(2,1)} async-done(((bf16[1,80,512]{2,1,0:T(8,128)(2,1)}), bf16[1,5120,512]{2,1,0:T(8,128)(2,1)}) %all-gather.6.cloned.1.call-update) | async-done | bytes 5242896 | tf_op jit(solution)/shard_map/all_gather | solution.py:22
  146.3 32.6 %convolution_bitcast_fusion = f32[5120,512]{0,1:T(8,128)} fusion(bf16[1024,5120]{1,0:T(8,128)(2,1)} %param.4, bf16[1,5120,512]{2,1,0:T(8,128)(2,1)} %all-gather.6.cloned.1.call-done), kind=kOutput, calls=%fused_computation.2 | convolution fusion | flops 10737942528 | bytes 26214400 | tf_op jit(solution)/shard_map/dot_general | solution.py:28
  178.9 11.4 %copy.14 = f32[5120,512]{1,0:T(8,128)} copy(f32[5120,512]{0,1:T(8,128)} %convolution_bitcast_fusion) | data formatting | bytes 20971520
  190.3 0.0 copy-start.1
  190.3 0.0 copy-start
  190.3 0.0 reduce-scatter.4.cloned.1.call-update
  190.3 0.0 all-gather.4.cloned.1.call-start
  190.4 0.7 all-gather.4.cloned.1.call-update
  191.1 0.1 copy-done.1
  191.2 11.0 %all_gather.11 = bf16[4096,80]{0,1:T(8,128)(2,1)S(1)} all-gather(bf16[1024,80]{0,1:T(8,128)(2,1)S(1)} %copy-done.1), channel_id=1, replica_groups=mesh['dp'=4,'fsdp'=64] {'dp'}, dimensions={0}, use_global_device_ids=true | all-gather | bytes 819200 | tf_op jit(solution)/shard_map/all_gather | solution.py:47
  202.2 0.1 convert_element_type.13
  202.3 324.4 %reduce-scatter.4.cloned.1.call-done = f32[80,512]{1,0:T(8,128)} async-done(((f32[5120,512]{1,0:T(8,128)}), f32[80,512]{1,0:T(8,128)}) %reduce-scatter.4.cloned.1.call-update) | async-done | bytes 163856 | tf_op jit(solution)/shard_map/reduce_scatter | solution.py:27
  526.8 0.9 broadcast_multiply_fusion
  527.7 0.0 copy-done
  527.7 0.2 multiply_reduce_fusion.1
  527.9 122.4 %psum.21 = f32[8]{0:T(128)S(1)} all-reduce(f32[8]{0:T(128)S(1)} %multiply_reduce_fusion.1), channel_id=1, replica_groups=mesh['dp'=4,'fsdp'=64] {'dp','fsdp'}, use_global_device_ids=true, to_apply=%region_2.0 | all-reduce | flops 8 | bytes 64 | tf_op jit(solution)/shard_map/psum | solution.py:39
  650.3 0.2 multiply_reduce_fusion
  650.5 1.6 multiply_reduce_fusion.2
  652.1 87.3 %psum.22 = f32[]{:T(128)} all-reduce(f32[]{:T(128)} %multiply_reduce_fusion.2), channel_id=1, replica_groups=mesh['dp'=4,'fsdp'=64] {'dp','fsdp'}, use_global_device_ids=true, to_apply=%region_5.0 | all-reduce | flops 1 | bytes 8 | tf_op jit(solution)/shard_map/psum | solution.py:41
  740.1 1.6 fusion.14
  741.7 0.0 all-gather.4.cloned.1.call-done
  741.7 5.7 fusion
  747.4 0.2 reshape.13
  747.6 0.2 reduce_sum.49
  747.9 74.1 %psum.23 = f32[128,9]{0,1:T(8,128)S(1)} all-reduce(f32[128,9]{0,1:T(8,128)S(1)} %multiply_bitcast_fusion), channel_id=1, replica_groups=mesh['dp'=4,'fsdp'=64] {'dp','fsdp'}, use_global_device_ids=true, to_apply=%region_8.0 | all-reduce | flops 1152 | bytes 9216 | tf_op jit(solution)/shard_map/psum | solution.py:59
  822.0 0.6 maximum_bitcast_fusion
  822.5 0.7 constant_dynamic-slice_fusion
  (2 shorter events, 0.0 us)
Async XLA Ops:
  7.2 139.2 %all-gather.6.cloned.1.call-start = ((), (), s32[]{:S(2)}) async-start(), calls=%async_computation.2 | async-start | bytes 5324800 | tf_op jit(solution)/shard_map/all_gather | solution.py:22
  9.3 517.5 %reduce-scatter.4.cloned.1.call-start = ((), (), s32[]{:S(2)}) async-start(), calls=%async_computation.3 | async-start | bytes 10649600 | tf_op jit(solution)/shard_map/reduce_scatter | solution.py:27
  190.3 0.9 copy-start.1
  190.3 337.4 %copy-start = (f32[8,80,512]{2,1,0:T(8,128)S(1)}, f32[8,80,512]{2,1,0:T(8,128)}, u32[]{:S(2)}) copy-start(f32[8,80,512]{2,1,0:T(8,128)} %param.7) | copy-start | bytes 3932164
  190.3 551.3 %all-gather.4.cloned.1.call-start = ((), (), s32[]{:S(2)}) async-start(), calls=%async_computation.1 | async-start | bytes 4259840 | tf_op jit(solution)/shard_map/all_gather | solution.py:48
Sparse Core Ops, SparseCore 0:
  12.3 134.0 all-gather.5
  190.5 336.2 reduce-scatter.3
  530.5 168.7 all-gather.3
where the time goes:
time: 830 us
  waiting for transfers between devices  462 us (56%)
  blocking collectives  295 us (36%)
  matrix products  38.3 us (5%)
  between operations  14.5 us (2%)
  local copies, waits for them, and re-layouts  13 us (2%)
    reduce_scatter x1, waiting for transfers between devices, local(): lax.psum_scatter(lax.dot_general(columns, image, (((0,), (0,)), ((), ()))...  324 us
    all_gather x1, waiting for transfers between devices, local(): lax.all_gather(narrow, 'fsdp', axis=0, tiled=True)  137 us
    psum x1, blocking collectives, local(): coeffs = lax.psum(local_products, ('dp', 'fsdp')) * mean_scale  122 us
    psum x1, blocking collectives, local(): beta = jnp.sqrt(lax.psum(jnp.sum(orth * orth), ('dp', 'fsdp')) * mean_scale)  87.3 us
    psum x1, blocking collectives, local(): totals = lax.psum(partial_value, ('dp', 'fsdp'))  74.1 us
    dot_general x1, matrix products, local(): lax.dot_general(columns, image, (((0,), (0,)), ((), ())), preferred_eleme...  32.6 us
  transfers between devices with their start and end apart: 3, of which 2 were waited for; matrix products, arithmetic and copies ran while one was open for 1% of the time, Pallas kernels for 0%

commit v1 on v0

v1 whole, which is shorter than its diff:
```python
import functools

import jax
import jax.numpy as jnp
from jax import lax
from jax.experimental import pallas as pl
from jax.experimental.pallas import tpu as pltpu
from jax.sharding import PartitionSpec as P

D = 2048
FF = 5120
TOKENS = 65536
EX_TOK = 32
K = 8
NZ, NY = 8, 4
BLK = 80
WID = 512
ROWS_A, ROWS_B = 32, 48
MESH = pl.DeviceIdType.MESH
BF = jnp.bfloat16
F32 = jnp.float32
SIGNS = (1, -1)


def half_of(sign):
    return 0 if sign > 0 else 1


def wrap(delta, size):
    delta %= size
    return delta - size if delta > size // 2 else delta


def parts_of(kind, hop, own):
    if hop == 1 and own:
        return ("o", "t")
    return ("f",)


def link_of(msg):
    kind = msg[0]
    if kind in ("Az", "az"):
        return ("z", msg[2])
    if kind in ("Ay", "ay", "Ry", "RY"):
        return ("y", msg[1])
    if kind in ("Bz", "bz", "Rz", "RZ"):
        return ("z", msg[1])
    if kind in ("By", "by"):
        return ("y", msg[2])
    if kind in ("qx", "vx", "hx", "xa", "xb", "hl"):
        return ("x", 0)
    return ("c", 0) if kind == "hc" else (kind, msg[1])


def kilobytes(msg):
    kind = msg[0]
    a, b = 2 * ROWS_A, 2 * ROWS_B
    if kind == "Ay":
        return a / 2 if msg[3] in ("o", "t") or msg[2] == 2 else a
    if kind == "Az":
        return a / 2 if msg[4] in ("o", "t") or msg[3] == 4 else a
    if kind == "Bz":
        return b / 2 if msg[3] in ("o", "t") or msg[2] == 4 else b
    if kind == "By":
        return b / 2 if msg[4] in ("o", "t") or msg[3] == 2 else b
    if kind == "az":
        return a / 2 if msg[3] == 4 else a
    if kind == "ay":
        return a / 2 if msg[2] == 2 else a
    if kind == "bz":
        return b / 2 if msg[2] == 4 else b
    if kind == "by":
        return b / 2 if msg[3] == 2 else b
    if kind == "Ry":
        return 16 if msg[2] == 2 else 32
    if kind == "Rz":
        return 16 if msg[2] == 4 else 32
    if kind == "RZ":
        return 64 if msg[2] == 4 else 128
    if kind == "RY":
        return 128 if msg[2] == 2 else 256
    return {"qx": 80, "vx": 560, "hx": 80, "hl": 160, "hc": 320, "xa": a, "xb": b}.get(kind, 8)


def build():
    tasks = {}

    def task(name, needs=(), after=(), cost=0.0, sends=()):
        needs, sends = list(needs), list(sends)
        tasks[name] = (needs, list(after), cost + 0.05 * len(needs) + 0.1 * len(sends), sends)

    first = []
    for s in SIGNS:
        first += [("Bz", s, 1), ("Ay", s, 1)]
    for s in SIGNS:
        first += [("Az", 0, s, 1), ("By", 0, s, 1)]
    task(
        ("start",),
        cost=0.5,
        sends=[("qx",)] + [m + ("o",) for m in first]
        + [("Rz", s, 1) for s in SIGNS] + [("Ry", s, 1) for s in SIGNS],
    )
    task(("qx",), [("qx",)], [("start",)], sends=[m + ("t",) for m in first])
    for s in SIGNS:
        task(
            ("Ay", s),
            [("Ay", s, 1, "o"), ("Ay", s, 1, "t")],
            [("qx",)],
            sends=[("Ay", s, 2, "f")] + [("Az", wrap(-s, NY), u, 1, "f") for u in SIGNS],
        )
    task(
        ("Ay2",),
        [("Ay", s, 2, "f") for s in SIGNS],
        [("Ay", s) for s in SIGNS],
        sends=[("Az", 2, u, 1, "f") for u in SIGNS],
    )
    for dy in (0, 1, -1, 2):
        for s in SIGNS:
            for h in (1, 2, 3):
                task(
                    ("Az", dy, s, h),
                    [("Az", dy, s, h, p) for p in parts_of("Az", h, dy == 0)],
                    sends=[("Az", dy, s, h + 1, "f")],
                )
    for s in SIGNS:
        for h in (1, 2, 3):
            task(
                ("Bz", s, h),
                [("Bz", s, h, p) for p in parts_of("Bz", h, True)],
                sends=[("Bz", s, h + 1, "f")] + [("By", wrap(-s * h, NZ), u, 1, "f") for u in SIGNS],
            )
    task(
        ("Bz4",), [("Bz", s, 4, "f") for s in SIGNS], sends=[("By", 4, u, 1, "f") for u in SIGNS]
    )
    for dz in range(-3, 5):
        for s in SIGNS:
            task(
                ("By", dz, s),
                [("By", dz, s, 1, p) for p in parts_of("By", 1, dz == 0)],
                sends=[("By", dz, s, 2, "f")],
            )
    late = [("Az", dy, s, 3) for dy in (0, 1, -1, 2) for s in SIGNS]
    late += [("By", dz, s) for dz in range(-3, 5) for s in SIGNS]
    for s in SIGNS:
        task(("Ry", s), [("Ry", s, 1)], sends=[("Ry", s, 2)])
        for h in (1, 2, 3):
            task(("Rz", s, h), [("Rz", s, h)], sends=[("Rz", s, h + 1)])
            task(("RZ", s, h), [("RZ", s, h)], sends=[("RZ", s, h + 1)])
        task(("RY", s), [("RY", s, 1)], sends=[("RY", s, 2)])
    task(
        ("RZ0",),
        [("Ry", s, 2) for s in SIGNS],
        [("Ry", s) for s in SIGNS] + late,
        sends=[("RZ", s, 1) for s in SIGNS],
    )
    task(
        ("RY0",),
        [("Rz", s, 4) for s in SIGNS],
        [("Rz", s, h) for s in SIGNS for h in (1, 2, 3)] + late,
        sends=[("RY", s, 1) for s in SIGNS],
    )
    task(("vx",), after=[("qx",)], cost=0.6, sends=[("vx",)])
    task(("hx",), after=[("qx",)], cost=1.0, sends=[("hx",)])
    task(("hl",), [("hx",)], [("hx",)], sends=[("hl",)])
    task(("hc",), [("hl",)], [("hl",)], sends=[("hc",)])
    task(("gram",), after=[("qx",)], cost=2.0)
    for g, planes in enumerate(PLANES):
        needs, after = [], [("m1", g - 1)] if g else [("load",)]
        for dz in planes:
            for s in SIGNS:
                needs.append(("By", dz, s, 2, "f"))
                after.append(("By", dz, s))
            if dz == 0:
                after += [("Ay", s) for s in SIGNS] + [("Ay2",)]
            elif dz == 4:
                needs += [("Az", dy, s, 4, "f") for dy in (0, 1, -1, 2) for s in SIGNS]
                after.append(("Bz4",))
            else:
                s = -1 if dz > 0 else 1
                after += [("Az", dy, s, abs(dz)) for dy in (0, 1, -1, 2)] + [("Bz", s, abs(dz))]
        task(("m1", g), needs, after, cost=1.1 * len(planes))
    task(("load",), after=[("start",)], cost=0.1)
    task(("img",), after=[("m1", len(PLANES) - 1)], cost=0.5)
    for n, dz in enumerate(ORDER):
        task(("m2", dz), after=[("img",)] + ([("m2", ORDER[n - 1])] if n else []), cost=0.95)
    for dy in (0, 1, -1, 2):
        task(("az", dy, 4), after=[("m2", 4)], cost=0.1, sends=[("az", dy, s, 4) for s in SIGNS])
        for s in SIGNS:
            for d in (3, 2, 1):
                task(
                    ("az", dy, s, d),
                    [("az", dy, s, d + 1)],
                    [("m2", s * d)],
                    cost=0.1,
                    sends=[("az", dy, s, d)],
                )
        task(("az", dy, 0), [("az", dy, s, 1) for s in SIGNS], [("m2", 0)], cost=0.15)
    task(("ay", 2), after=[("az", 2, 0)], cost=0.1, sends=[("ay", s, 2) for s in SIGNS])
    for s in SIGNS:
        task(("ay", s, 1), [("ay", s, 2)], [("az", s, 0)], cost=0.1, sends=[("ay", s, 1)])
    task(
        ("xa",), [("ay", s, 1) for s in SIGNS], [("az", 0, 0)], cost=0.15, sends=[("xa",)]
    )
    for dz in range(-3, 5):
        task(("by", dz, 2), after=[("m2", dz)], cost=0.1, sends=[("by", dz, s, 2) for s in SIGNS])
        for s in SIGNS:
            task(
                ("by", dz, s, 1),
                [("by", dz, s, 2)],
                [("m2", dz)],
                cost=0.15,
                sends=[("by", dz, s, 1)],
            )
        task(("by", dz, 0), [("by", dz, s, 1) for s in SIGNS], [("m2", dz)], cost=0.2)
    task(("bz", 4), after=[("by", 4, 0)], cost=0.1, sends=[("bz", s, 4) for s in SIGNS])
    for s in SIGNS:
        for d in (3, 2, 1):
            task(
                ("bz", s, d),
                [("bz", s, d + 1)],
                [("by", s * d, 0)],
                cost=0.15,
                sends=[("bz", s, d)],
            )
    task(("xb",), [("bz", s, 1) for s in SIGNS], [("by", 0, 0)], cost=0.2, sends=[("xb",)])
    for k in range(4):
        needs, after = [], [("m2", ORDER[-1])]
        if k == 0:
            needs += [("RZ", s, 4) for s in SIGNS] + [("RY", s, 2) for s in SIGNS]
            needs += [("hc",), ("vx",)]
            after += [("RZ", s, h) for s in SIGNS for h in (1, 2, 3)] + [("RY", s) for s in SIGNS]
            after += [("RZ0",), ("RY0",), ("hc",), ("vx",), ("gram",)]
        else:
            after += [("p8", k - 1)]
        task(("p8", k), needs, after, cost=1.3)
    task(("g1",), after=[("p8", 3)], cost=0.1, sends=[("g1z", k) for k in range(1, NZ)])
    task(
        ("g2",), [("g1z", k) for k in range(1, NZ)], [("g1",)], 0.1, [("g1y", k) for k in range(1, NY)]
    )
    task(
        ("g3",), [("g1y", k) for k in range(1, NY)], [("g2",)], 0.1, [("g1x", k) for k in range(1, 8)]
    )
    return tasks


PLANES = ((0,), (1, -1), (2, -2), (3, -3), (4,))
ORDER = (4, 3, -3, 2, -2, 1, -1, 0)


def schedule(tasks):
    rate = {"z": 46.0, "y": 46.0, "x": 45.0, "c": 400.0}
    delay = {"z": 1.5, "y": 1.5, "x": 2.0, "c": 0.8}
    waits = {}
    followers = {name: [] for name in tasks}
    for name, (needs, after, _, _) in tasks.items():
        for msg in needs:
            waits.setdefault(msg, []).append(name)
        for other in after:
            followers[other].append(name)

    def cost_of(msg):
        axis = link_of(msg)[0]
        return kilobytes(msg) / rate.get(axis, 40.0) + delay.get(axis, 3.0)

    @functools.cache
    def rank(name):
        _, _, cost, sends = tasks[name]
        rest = [rank(f) for f in followers[name]]
        rest += [cost_of(m) + max([rank(w) for w in waits.get(m, ())], default=0) for m in sends]
        return cost + max(rest, default=0)

    now, free, arrives, done, order = 0.0, {}, {}, {}, []
    left = dict(tasks)
    while left:
        ready, soonest = [], None
        for name, (needs, after, _, _) in left.items():
            if any(a not in done for a in after) or any(m not in arrives for m in needs):
                continue
            at = max([arrives[m] for m in needs], default=0.0)
            if at <= now:
                ready.append((-rank(name), at, name))
            else:
                soonest = at if soonest is None else min(soonest, at)
        if not ready:
            now = soonest
            continue
        name = min(ready, key=lambda r: (r[0], r[1]))[2]
        _, _, cost, sends = left.pop(name)
        now += cost
        done[name] = now
        order.append(name)
        for msg in sends:
            link = link_of(msg)
            axis = link[0]
            begin = max(now, free.get(link, 0.0))
            free[link] = begin + kilobytes(msg) / rate.get(axis, 40.0)
            arrives[msg] = free[link] + delay.get(axis, 3.0)
    return order, done, arrives


def product(a, b, ca, cb):
    return lax.dot_general(a, b, (((ca,), (cb,)), ((), ())), preferred_element_type=F32)


def kernel(
    order, tasks, index,
    x_hbm, hid_ref, res_ref, basis_ref,
    new_ref, hess_ref, proj_ref,
    xv, q, p, send_a, send_b, recv_a, recv_b, acc, img, r, v16, ht, hs, cur,
    early, late, gz, gy, gx, square, load_sem, send_sem, recv_sem,
):
    dp, fs = lax.axis_index("dp"), lax.axis_index("fsdp")
    z, y, xh = fs // 8, lax.rem(fs // 2, 4), lax.rem(fs, 2)
    xl, core = dp // 2, lax.rem(dp, 2)
    other = 1 - xh

    zi = {d: lax.rem(z + (d + NZ), NZ) for d in range(-3, 8)}
    zi[-4] = zi[4]
    yi = {d: lax.rem(y + (d + NY), NY) for d in range(-1, 4)}
    yi[-2] = yi[2]

    def fsdp(za, ya, xa):
        return (za * NY + ya) * 2 + xa

    def along_z(d):
        return (dp, fsdp(zi[d], y, xh))

    def along_y(d):
        return (dp, fsdp(z, yi[d], xh))

    def along_x(k):
        xa = 1 - xh if k & 4 else xh
        la = 1 - xl if k & 2 else xl
        ca = 1 - core if k & 1 else core
        return (la * 2 + ca, fsdp(z, y, xa))

    partners = [along_z(d) for d in range(1, NZ)] + [along_y(d) for d in range(1, NY)]
    partners += [along_x(k) for k in range(1, 8)]

    loading = pltpu.make_async_copy(x_hbm, xv, load_sem)
    loading.start()
    barrier = pltpu.get_barrier_semaphore()
    for device in partners:
        pl.semaphore_signal(barrier, inc=1, device_id=device, device_id_type=MESH)

    def q_part(rows, part, oz, oy):
        at = q.at[zi[oz], yi[oy]]
        which = {"f": slice(None), "o": xh, "t": other}.get(part, part)
        return at.at[which, rows]

    a_rows, b_rows = pl.ds(0, ROWS_A), pl.ds(ROWS_A, ROWS_B)

    def slot_a(msg):
        if msg[0] == "az":
            _, dy, s, d = msg
            base = {0: 0, 1: 7, -1: 14, 2: 21}[dy]
            return base + (6 if d == 4 else (d - 1) * 2 + half_of(s)), d == 4, s
        if msg[0] == "ay":
            _, s, d = msg
            return 28 + (2 if d == 2 else half_of(s)), d == 2, s
        return 31, False, 1

    def slot_b(msg):
        if msg[0] == "by":
            _, dz, s, d = msg
            return (dz + 3) * 3 + (2 if d == 2 else half_of(s)), d == 2, s
        if msg[0] == "bz":
            _, s, d = msg
            return 24 + (6 if d == 4 else (d - 1) * 2 + half_of(s)), d == 4, s
        return 31, False, 1

    def piece(buf, slot):
        n, halved, s = slot
        return buf.at[n, half_of(s)] if halved else buf.at[n]

    def place(msg):
        kind = msg[0]
        if kind == "qx":
            here = q.at[z, y, xh]
            return here, here, q.at[z, y, other], along_x(4)
        if kind in ("Ay", "Az", "Bz", "By"):
            rows = a_rows if kind[0] == "A" else b_rows
            if kind in ("Ay", "Bz"):
                _, s, h, part = msg
            else:
                _, off, s, h, part = msg
            size = NZ if kind[1] == "z" else NY
            if h == size // 2:
                part = half_of(s)
            if kind[1] == "y":
                oz = off if kind == "By" else 0
                here = q_part(rows, part, oz, wrap(-s * (h - 1), NY))
                there = q_part(rows, part, oz, wrap(-s * h, NY))
                return here, here, there, along_y(s)
            oy = off if kind == "Az" else 0
            here = q_part(rows, part, wrap(-s * (h - 1), NZ), oy)
            there = q_part(rows, part, wrap(-s * h, NZ), oy)
            return here, here, there, along_z(s)
        if kind in ("Ry", "RZ", "Rz", "RY"):
            _, s, h = msg
            last = h == (NY if kind[1] in "yY" else NZ) // 2
            low = 0 if kind in ("Ry", "RZ") else 32
            rows = pl.ds(low + 16 * half_of(s), 16) if last else pl.ds(low, 32)
            n = NY if kind[1] in "yY" else NZ
            a, b = wrap(-s * (h - 1), n), wrap(-s * h, n)
            if kind == "Ry":
                here, there = r.at[z, yi[a], rows], r.at[z, yi[b], rows]
            elif kind == "Rz":
                here, there = r.at[zi[a], y, rows], r.at[zi[b], y, rows]
            elif kind == "RZ":
                here, there = r.at[zi[a], :, rows], r.at[zi[b], :, rows]
            else:
                here, there = r.at[:, yi[a], rows], r.at[:, yi[b], rows]
            return here, here, there, along_y(s) if n == NY else along_z(s)
        if kind == "vx":
            here = v16.at[pl.ds(0, K - 1), xh]
            return here, here, v16.at[pl.ds(0, K - 1), other], along_x(4)
        if kind == "hx":
            return hs, ht.at[xl, core, xh], ht.at[xl, core, other], along_x(4)
        if kind == "hl":
            here = ht.at[xl, core]
            return here, here, ht.at[1 - xl, core], along_x(2)
        if kind == "hc":
            here = ht.at[:, core]
            return here, here, ht.at[:, 1 - core], along_x(1)
        if kind in ("az", "ay", "xa"):
            slot = slot_a(msg)
            target = piece(recv_a, slot)
            src = piece(send_a, slot)
        elif kind in ("by", "bz", "xb"):
            slot = slot_b(msg)
            target = piece(recv_b, slot)
            src = piece(send_b, slot)
        if kind in ("xa", "xb"):
            return src, target, target, along_x(4)
        if kind in ("az", "by"):
            return src, target, target, along_z(msg[2]) if kind == "az" else along_y(msg[2])
        if kind in ("ay", "bz"):
            return src, target, target, along_y(msg[1]) if kind == "ay" else along_z(msg[1])
        lane, k = int(kind[1]) - 1, msg[1]
        if kind[2] == "z":
            return gz.at[lane, z], gz.at[lane, z], gz.at[lane, zi[-k + NZ if k > 3 else -k]], along_z(k)
        if kind[2] == "y":
            return gy.at[lane, y], gy.at[lane, y], gy.at[lane, yi[-k + NY if k > 1 else -k]], along_y(k)
        mine = xh * 4 + xl * 2 + core
        xa = 1 - xh if k & 4 else xh
        la = 1 - xl if k & 2 else xl
        ca = 1 - core if k & 1 else core
        return gx.at[lane, mine], gx.at[lane, mine], gx.at[lane, xa * 4 + la * 2 + ca], along_x(k)

    started = []

    def send(msg):
        src, target, _, device = place(msg)
        n = index[msg]
        copy = pltpu.make_async_remote_copy(
            src_ref=src, dst_ref=target, send_sem=send_sem.at[n], recv_sem=recv_sem.at[n],
            device_id=device, device_id_type=MESH,
        )
        copy.start()
        started.append(copy)

    def receive(msg):
        _, _, lands, device = place(msg)
        n = index[msg]
        pltpu.make_async_remote_copy(
            src_ref=lands, dst_ref=lands, send_sem=send_sem.at[n], recv_sem=recv_sem.at[n],
            device_id=device, device_id_type=MESH,
        ).wait_recv()

    def fold(rows, buf, where, slots, out):
        for k in (0, 1):
            total = p[where[0], where[1], k, rows]
            for n, halved, s in slots:
                if not halved or half_of(s) == k:
                    total = total + buf[n, k].astype(F32)
            if out is None:
                p[where[0], where[1], k, rows] = total
            else:
                out[0][out[1], k] = total.astype(BF)

    def fold_a(where, msgs, out=None):
        fold(a_rows, recv_a, where, [slot_a(m) for m in msgs], out and (send_a, slot_a(out)[0]))

    def fold_b(where, msgs, out=None):
        fold(b_rows, recv_b, where, [slot_b(m) for m in msgs], out and (send_b, slot_b(out)[0]))

    def lanes_of(plane):
        return pl.ds(pl.multiple_of(plane * (NY * 2 * BLK), 128), NY * 2 * BLK)

    def per_token(rows, k):
        errors = r[2 * k : 2 * k + 2].reshape(512, WID)
        hidden = ht[k // 2, k % 2].reshape(2 * BLK, 512).astype(F32)
        mapped = product(rows, errors, 1, 1)
        n = rows.shape[0] // (2 * BLK)
        return jnp.sum(mapped.reshape(n, 2 * BLK, 512) * hidden[None], axis=1)

    def per_example(tokens, k):
        t = lax.broadcasted_iota(jnp.int32, (512, 128), 0)
        e = lax.broadcasted_iota(jnp.int32, (512, 128), 1)
        owner = 32 * k + (t // 64) * 4 + 2 * xh + lax.rem(t, 64) // EX_TOK
        marks = jnp.where(owner == e, 1.0, 0.0).astype(F32)
        return jnp.dot(tokens, marks, precision=lax.Precision.HIGHEST, preferred_element_type=F32)

    def work(name):
        kind = name[0]
        if kind == "start":
            narrow = basis_ref[K - 1].astype(BF)
            q[z, y, xh] = narrow
            v16[K - 1, xh] = narrow
            r[z, y] = res_ref[...]
            pl.semaphore_wait(barrier, len(partners))
        elif kind == "vx":
            for n in range(K - 1):
                v16[n, xh] = basis_ref[n].astype(BF)
            v16[K - 1, other] = q[z, y, other]
        elif kind == "hx":
            eye_a = lax.broadcasted_iota(jnp.int32, (BLK, BLK), 0)
            eye_b = lax.broadcasted_iota(jnp.int32, (BLK, BLK), 1)
            eye = jnp.where(eye_a == eye_b, 1.0, 0.0).astype(BF)

            def turned(which):
                rows = [hid_ref[pl.ds(pl.multiple_of((2 * n + which) * 64, 64), 64), :] for n in range(8)]
                return product(eye, jnp.concatenate(rows, axis=0), 1, 1).astype(BF)

            ht[xl, core, xh] = turned(xh)
            hs[...] = turned(other)
        elif kind == "gram":
            lane = lax.broadcasted_iota(jnp.int32, (8, 128), 1)
            table = jnp.zeros((8, 128), F32)
            for i in range(K):
                rows = [jnp.sum(basis_ref[j] * basis_ref[i], axis=0, keepdims=True) for j in range(K)]
                column = jnp.sum(jnp.concatenate(rows, axis=0), axis=1, keepdims=True)
                table = table + jnp.where(lane == i, column, 0.0)
            early[8:16] = table
            early[0:8] = jnp.zeros((8, 128), F32)
        elif kind == "load":
            loading.wait()
        elif kind == "m1":
            total = None
            for dz in PLANES[name[1]]:
                term = product(xv[:, lanes_of(zi[dz])], q[zi[dz]].reshape(NY * 2 * BLK, WID), 1, 0)
                total = term if total is None else total + term
            acc[...] = total if name[1] == 0 else acc[...] + total
        elif kind == "img":
            img[...] = acc[...].astype(BF)
        elif kind == "m2":
            plane = zi[name[1]]
            p[plane] = product(xv[:, lanes_of(plane)], img[...], 0, 0).reshape(NY, 2, BLK, WID)
        elif kind == "az":
            dy = name[1]
            if name[2] == 4:
                fold_a((zi[4], yi[dy]), [], ("az", dy, 1, 4))
            elif name[2] == 0:
                fold_a((z, yi[dy]), [("az", dy, s, 1) for s in SIGNS])
            else:
                s, d = name[2:]
                fold_a((zi[s * d], yi[dy]), [("az", dy, s, d + 1)], ("az", dy, s, d))
        elif kind == "ay":
            if name[1] == 2 and len(name) == 2:
                fold_a((z, yi[2]), [], ("ay", 1, 2))
            else:
                s = name[1]
                fold_a((z, yi[s]), [("ay", s, 2)], ("ay", s, 1))
        elif kind == "xa":
            fold_a((z, y), [("ay", s, 1) for s in SIGNS])
            fold_a((z, y), [], ("xa",))
        elif kind == "by":
            dz = name[1]
            if len(name) == 4:
                s = name[2]
                fold_b((zi[dz], yi[s]), [("by", dz, s, 2)], ("by", dz, s, 1))
            elif name[2] == 2:
                fold_b((zi[dz], yi[2]), [], ("by", dz, 1, 2))
            else:
                fold_b((zi[dz], y), [("by", dz, s, 1) for s in SIGNS])
        elif kind == "bz":
            if len(name) == 2:
                fold_b((zi[4], y), [], ("bz", 1, 4))
            else:
                s, d = name[1:]
                fold_b((zi[s * d], y), [("bz", s, d + 1)], ("bz", s, d))
        elif kind == "xb":
            fold_b((z, y), [("bz", s, 1) for s in SIGNS])
            fold_b((z, y), [], ("xb",))
        elif kind == "p8":
            k = name[1]
            early[0:8] = early[0:8] + per_example(per_token(v16[...].reshape(K * 2 * BLK, WID), k), k)
        elif kind == "g1":
            gz[0, z] = early[...]
        elif kind == "g2":
            gy[0, y] = ring_sum(gz, 0, NZ)
        elif kind == "g3":
            gx[0, xh * 4 + xl * 2 + core] = ring_sum(gy, 0, NY)

    def ring_sum(buf, lane, n):
        total = buf[lane, 0]
        for k in range(1, n):
            total = total + buf[lane, k]
        return total

    for name in order:
        needs, _, _, sends = tasks[name]
        if name[0] != "start":
            for msg in needs:
                receive(msg)
        work(name)
        for msg in sends:
            send(msg)

    receive(("xa",))
    receive(("xb",))
    mean = 1.0 / (FF * D)
    for k in (0, 1):
        cur[k, a_rows] = (p[z, y, k, a_rows] + recv_a[31, k].astype(F32)) * (1.0 / TOKENS)
        cur[k, b_rows] = (p[z, y, k, b_rows] + recv_b[31, k].astype(F32)) * (1.0 / TOKENS)
    mine = cur[xh]
    rows = [jnp.sum(basis_ref[n] * mine, axis=0, keepdims=True) for n in range(K)]
    rows.append(jnp.sum(mine * mine, axis=0, keepdims=True))
    rows.append(jnp.zeros((7, WID), F32))
    sums = jnp.sum(jnp.concatenate(rows, axis=0), axis=1, keepdims=True)
    late[...] = jnp.broadcast_to(sums, (16, 128))
    both = cur[...].reshape(2 * BLK, WID)
    high = both.astype(BF)
    low = (both - high.astype(F32)).astype(BF)
    pair = jnp.concatenate([high, low], axis=0)
    shown = jnp.zeros((1, 128), F32)
    for k in range(4):
        tokens = per_token(pair, k)
        tokens = tokens[0:1] + tokens[1:2]
        shown = shown + per_example(jnp.broadcast_to(tokens, (8, 512)), k)[0:1]
    late[9:10] = shown

    gz[1, z] = late[...]
    for k in range(1, NZ):
        send(("g2z", k))
    for k in range(1, 8):
        receive(("g1x", k))
    first = ring_sum(gx, 0, 8)
    for k in range(1, NZ):
        receive(("g2z", k))
    gy[1, y] = ring_sum(gz, 1, NZ)
    for k in range(1, NY):
        send(("g2y", k))
    for k in range(1, NY):
        receive(("g2y", k))
    gx[1, xh * 4 + xl * 2 + core] = ring_sum(gy, 1, NY)
    for k in range(1, 8):
        send(("g2x", k))
    for k in range(1, 8):
        receive(("g2x", k))
    second = ring_sum(gx, 1, 8)

    coeff = second[0:8] * mean
    squared = second[8:9] * mean
    sub = lax.broadcasted_iota(jnp.int32, (8, 128), 0)
    lane = lax.broadcasted_iota(jnp.int32, (8, 128), 1)
    row = jnp.sum(jnp.where(sub == lane, coeff, 0.0), axis=0, keepdims=True)
    cross = jnp.sum(coeff * first[8:16], axis=0, keepdims=True) * row
    cross = jnp.sum(cross, axis=1, keepdims=True) * mean
    twice = 2.0 * jnp.sum(coeff * coeff, axis=0, keepdims=True)
    beta = jnp.sqrt(jnp.maximum(squared - twice + cross, squared * 1e-12))
    inverse = 1.0 / beta
    lane1 = lax.broadcasted_iota(jnp.int32, (1, 128), 1)
    hess_ref[...] = jnp.where(lane1 == K, beta, row)[:, 0 : K + 1]
    left = mine
    for n in range(K):
        left = left - coeff[n : n + 1, 0:1] * basis_ref[n]
    new_ref[0] = left * inverse[:, 0:1]
    last = (second[9:10] - jnp.sum(coeff * first[0:8], axis=0, keepdims=True)) * inverse
    scale = (FF * D) ** (-0.5)
    square[...] = jnp.zeros((128, 128), F32)
    square[0:8] = first[0:8] * scale
    square[8:9] = last * scale
    square[...] = square[...].T
    proj_ref[...] = square[pl.ds(pl.multiple_of(dp * 32, 32), 32), 0 : K + 1]
    for copy in started:
        copy.wait_send()


def local(train_hidden, index_hidden, index_resid, basis):
    tasks = build()
    order, _, _ = schedule(tasks)
    messages = [m for name in tasks for m in tasks[name][3]]
    messages += [("g2z", k) for k in range(1, NZ)] + [("g2y", k) for k in range(1, NY)]
    messages += [("g2x", k) for k in range(1, 8)]
    index = {m: n for n, m in enumerate(messages)}
    vmem = pltpu.VMEM
    whole = pl.BlockSpec(memory_space=pltpu.VMEM)
    call = pl.pallas_call(
        functools.partial(kernel, order, tasks, index),
        out_shape=(
            jax.ShapeDtypeStruct((1, BLK, WID), F32),
            jax.ShapeDtypeStruct((1, K + 1), F32),
            jax.ShapeDtypeStruct((32, K + 1), F32),
        ),
        in_specs=[pl.BlockSpec(memory_space=pl.ANY), whole, whole, whole],
        out_specs=(whole, whole, whole),
        scratch_shapes=[
            vmem((1024, FF), BF),
            vmem((NZ, NY, 2, BLK, WID), BF),
            vmem((NZ, NY, 2, BLK, WID), F32),
            vmem((32, 2, ROWS_A, WID), BF),
            vmem((32, 2, ROWS_B, WID), BF),
            vmem((32, 2, ROWS_A, WID), BF),
            vmem((32, 2, ROWS_B, WID), BF),
            vmem((1024, WID), F32),
            vmem((1024, WID), BF),
            vmem((NZ, NY, 64, WID), BF),
            vmem((K, 2, BLK, WID), BF),
            vmem((2, 2, 2, BLK, WID), BF),
            vmem((BLK, WID), BF),
            vmem((2, BLK, WID), F32),
            vmem((16, 128), F32),
            vmem((16, 128), F32),
            vmem((2, NZ, 16, 128), F32),
            vmem((2, NY, 16, 128), F32),
            vmem((2, 8, 16, 128), F32),
            vmem((128, 128), F32),
            pltpu.SemaphoreType.DMA,
            pltpu.SemaphoreType.DMA((len(messages),)),
            pltpu.SemaphoreType.DMA((len(messages),)),
        ],
        compiler_params=pltpu.CompilerParams(
            collective_id=0, has_side_effects=True, vmem_limit_bytes=60 * 2**20
        ),
        cost_estimate=pl.CostEstimate(
            flops=14 * 10**9, bytes_accessed=13 * 10**6, transcendentals=0
        ),
        name="arnoldi",
    )
    return call(train_hidden, index_hidden, index_resid, basis)


def solution(mesh):
    in_specs = (P("fsdp", None), P("dp", "fsdp"), P("fsdp", "dp"), P(None, "fsdp", "dp"))
    out_specs = (P(None, "fsdp", "dp"), P(), P("dp", None))
    return jax.shard_map(local, mesh=mesh, in_specs=in_specs, out_specs=out_specs, check_vma=False)
```

time: 830 us -> 125 us (0.15)
  waiting for transfers between devices: 462 us -> 0 us
  blocking collectives: 295 us -> 0 us
  Pallas kernels: 0 us -> 118 us
  matrix products: 38.3 us -> 0 us
  between operations: 14.5 us -> 0.64 us
    reduce_scatter x1 -> x0, waiting for transfers between devices: 324 us -> none  [local(): lax.psum_scatter(lax.dot_general(columns, image, (((0,), (0,)), ((), ()))...]
    psum x3 -> x0, blocking collectives: 284 us -> none  [the longest x1 122 us: local(): coeffs = lax.psum(local_products, ('dp', 'fsdp')) * mean_scale]
    all_gather x2 -> x0, waiting for transfers between devices: 137 us -> none  [the longest x1 137 us: local(): lax.all_gather(narrow, 'fsdp', axis=0, tiled=True)]
    pallas_call x0 -> x1, Pallas kernels: none -> 118 us  [local(): return call(train_hidden, index_hidden, index_resid, basis)]
    dot_general x2 -> x0, matrix products: 38.3 us -> none  [the longest x1 32.6 us: local(): lax.dot_general(columns, image, (((0,), (0,)), ((), ())), preferred_eleme...]
    all_gather x1 -> x0, blocking collectives: 11 us -> none  [local(): every_hidden = lax.all_gather(index_hidden, 'dp', axis=0, tiled=True)]
  transfers between devices with their start and end apart: 3 -> 0, of which waited for: 2 -> 0; matrix products, arithmetic and copies ran while one was open for 1% -> 0% of each run, Pallas kernels for 0% -> 0%
where the time goes in v1:
time: 125 us; the launch traced here: 124 us
  Pallas kernels  118 us (94%)
  local copies, waits for them, and re-layouts  5.91 us (5%)
    pallas_call x1, Pallas kernels, local(): return call(train_hidden, index_hidden, index_resid, basis)  118 us
    unnamed x3, local copies, waits for them, and re-layouts  4.51 us

profile of v1, /device:TPU:1, one launch (start us, length us, event | category | flops | bytes accessed | tf_op | source)
XLA Modules:
  0.0 124.4 jit_solution(12818727866802760008)
XLA Ops:
  0.6 1.7 %copy.7.hid_ref = bf16[1024,80]{1,0:T(8,128)(2,1)} copy(bf16[1024,80]{0,1:T(8,128)(2,1)} %param.5) | data formatting | bytes 327680 | tf_op args[1]
  2.4 117.9 %arnoldi.1 = (f32[1,80,512]{2,1,0:T(8,128)}, f32[1,9]{1,0:T(1,128)}, f32[32,9]{1,0:T(8,128)}) custom-call(bf16[1024,5120]{1,0:T(8,128)(2,1)} %x_hbm.1, bf16[1024,80]{1,0:T(8,128)(2,1)} %copy.7.hid_ref, bf16[64,512]{1,0:T(8,128)(2,1)} %res_ref.1, f32[8,80,512]{2,1,0:T(8,128)} %basis_ref.1), custom_call_target="tpu_custom_call" | custom-call | flops 14000000000 | bytes 13000000 | tf_op jit(solution)/shard_map/arnoldi/pallas_call | solution.py:732
  120.3 1.4 %copy.8 = f32[32,9]{0,1:T(8,128)} copy(f32[32,9]{1,0:T(8,128)} %get-tuple-element.5) | data formatting | bytes 2304 | tf_op jit(solution)/shard_map/arnoldi/pallas_call | solution.py:732
  121.7 1.6 %copy.11 = f32[1,80,512]{2,1,0:T(8,128)} copy(f32[1,80,512]{2,1,0:T(8,128)} %get-tuple-element.9) | data formatting | bytes 327680
  123.3 1.2 copy.12

commit v2 on v1

--- a/solution.py
+++ b/solution.py
@@ -15,11 +15,15 @@
 NZ, NY = 8, 4
 BLK = 80
 WID = 512
-ROWS_A, ROWS_B = 32, 48
+ROWS_A, ROWS_B, ROWS_C = 32, 32, 16
 MESH = pl.DeviceIdType.MESH
 BF = jnp.bfloat16
 F32 = jnp.float32
 SIGNS = (1, -1)
+FAR = (4, 3, 5, 2, 6, 1, 7)
+WIDE = sorted(
+    range(1, 32), key=lambda k: -(min(k // 8, 4 - k // 8) + (0, 1, 2, 1)[(k >> 1) & 3]) * 2 - (k & 1)
+)
 
 
 def half_of(sign):
@@ -41,13 +45,13 @@
     kind = msg[0]
     if kind in ("Az", "az"):
         return ("z", msg[2])
-    if kind in ("Ay", "ay", "Ry", "RY"):
+    if kind in ("Ay", "ay", "Ry", "RY", "Cy"):
         return ("y", msg[1])
-    if kind in ("Bz", "bz", "Rz", "RZ"):
+    if kind in ("Bz", "bz", "Rz", "RZ", "Cz", "cz"):
         return ("z", msg[1])
-    if kind in ("By", "by"):
+    if kind in ("By", "by", "cy"):
         return ("y", msg[2])
-    if kind in ("qx", "vx", "hx", "xa", "xb", "hl"):
+    if kind in ("qx", "vx", "hx", "xa", "xb", "xc", "hl", "Cx", "cx"):
         return ("x", 0)
     return ("c", 0) if kind == "hc" else (kind, msg[1])
 
@@ -71,15 +75,16 @@
         return b / 2 if msg[2] == 4 else b
     if kind == "by":
         return b / 2 if msg[3] == 2 else b
-    if kind == "Ry":
-        return 16 if msg[2] == 2 else 32
-    if kind == "Rz":
-        return 16 if msg[2] == 4 else 32
-    if kind == "RZ":
-        return 64 if msg[2] == 4 else 128
-    if kind == "RY":
-        return 128 if msg[2] == 2 else 256
-    return {"qx": 80, "vx": 560, "hx": 80, "hl": 160, "hc": 320, "xa": a, "xb": b}.get(kind, 8)
+    if kind in ("Ry", "Rz", "RZ", "RY", "Cz", "Cy"):
+        full = {"Ry": 16, "Rz": 48, "RZ": 64, "RY": 384, "Cz": ROWS_C, "Cy": 8 * ROWS_C}[kind]
+        return full / 2 if msg[2] == (4 if kind[1] in "zZ" else 2) else full
+    if kind == "cz":
+        return ROWS_C / 2 if msg[2] == 4 else ROWS_C
+    if kind == "cy":
+        return 2 * ROWS_C if msg[3] == 2 else 4 * ROWS_C
+    if kind in ("Cx", "cx"):
+        return (8 if kind == "Cx" else 4) * ROWS_C
+    return {"qx": 64, "xc": ROWS_C, "vx": 560, "hx": 80, "hl": 160, "hc": 320, "xa": a, "xb": b}.get(kind, 8)
 
 
 def build():
@@ -87,7 +92,7 @@
 
     def task(name, needs=(), after=(), cost=0.0, sends=()):
         needs, sends = list(needs), list(sends)
-        tasks[name] = (needs, list(after), cost + 0.05 * len(needs) + 0.1 * len(sends), sends)
+        tasks[name] = (needs, list(after), cost + 0.01 * (len(needs) + len(sends)), sends)
 
     first = []
     for s in SIGNS:
@@ -97,7 +102,7 @@
     task(
         ("start",),
         cost=0.5,
-        sends=[("qx",)] + [m + ("o",) for m in first]
+        sends=[("qx",)] + [("Cz", s, 1) for s in SIGNS] + [m + ("o",) for m in first]
         + [("Rz", s, 1) for s in SIGNS] + [("Ry", s, 1) for s in SIGNS],
     )
     task(("qx",), [("qx",)], [("start",)], sends=[m + ("t",) for m in first])
@@ -139,6 +144,17 @@
                 [("By", dz, s, 1, p) for p in parts_of("By", 1, dz == 0)],
                 sends=[("By", dz, s, 2, "f")],
             )
+    for s in SIGNS:
+        for h in (1, 2, 3):
+            task(("Cz", s, h), [("Cz", s, h)], sends=[("Cz", s, h + 1)])
+        task(("Cy", s), [("Cy", s, 1)], sends=[("Cx", wrap(-s, NY)), ("Cy", s, 2)])
+    task(
+        ("CY0",),
+        [("Cz", s, 4) for s in SIGNS],
+        [("Cz", s, h) for s in SIGNS for h in (1, 2, 3)],
+        sends=[("Cx", 0)] + [("Cy", s, 1) for s in SIGNS],
+    )
+    task(("Cy2",), [("Cy", s, 2) for s in SIGNS], [("Cy", s) for s in SIGNS], sends=[("Cx", 2)])
     late = [("Az", dy, s, 3) for dy in (0, 1, -1, 2) for s in SIGNS]
     late += [("By", dz, s) for dz in range(-3, 5) for s in SIGNS]
     for s in SIGNS:
@@ -159,13 +175,13 @@
         [("Rz", s, h) for s in SIGNS for h in (1, 2, 3)] + late,
         sends=[("RY", s, 1) for s in SIGNS],
     )
-    task(("vx",), after=[("qx",)], cost=0.6, sends=[("vx",)])
-    task(("hx",), after=[("qx",)], cost=1.0, sends=[("hx",)])
+    task(("vx",), after=[("qx",), ("Cy2",)], cost=0.1, sends=[("vx",)])
+    task(("hx",), after=[("vx",)], sends=[("hx",)])
     task(("hl",), [("hx",)], [("hx",)], sends=[("hl",)])
     task(("hc",), [("hl",)], [("hl",)], sends=[("hc",)])
     task(("gram",), after=[("qx",)], cost=2.0)
     for g, planes in enumerate(PLANES):
-        needs, after = [], [("m1", g - 1)] if g else [("load",)]
+        needs, after = [], [("m1", g - 1)] if g else [("load",), ("CY0",), ("Cy2",)]
         for dz in planes:
             for s in SIGNS:
                 needs.append(("By", dz, s, 2, "f"))
@@ -180,49 +196,77 @@
                 after += [("Az", dy, s, abs(dz)) for dy in (0, 1, -1, 2)] + [("Bz", s, abs(dz))]
         task(("m1", g), needs, after, cost=1.1 * len(planes))
     task(("load",), after=[("start",)], cost=0.1)
-    task(("img",), after=[("m1", len(PLANES) - 1)], cost=0.5)
+    for k in range(4):
+        task(("xs", k), after=[("load",)] + ([("xs", k - 1)] if k else []), cost=0.7)
+    task(
+        ("m1c",),
+        [("Cx", dy) for dy in (0, 1, -1, 2)],
+        [("CY0",), ("Cy2",), ("m1", 0), ("xs", 3)],
+        cost=0.9,
+    )
+    task(("img",), after=[("m1", len(PLANES) - 1), ("m1c",)], cost=0.5)
     for n, dz in enumerate(ORDER):
         task(("m2", dz), after=[("img",)] + ([("m2", ORDER[n - 1])] if n else []), cost=0.95)
     for dy in (0, 1, -1, 2):
-        task(("az", dy, 4), after=[("m2", 4)], cost=0.1, sends=[("az", dy, s, 4) for s in SIGNS])
+        task(("az", dy, 4), after=[("m2", 4)], cost=0.04, sends=[("az", dy, s, 4) for s in SIGNS])
         for s in SIGNS:
             for d in (3, 2, 1):
                 task(
                     ("az", dy, s, d),
                     [("az", dy, s, d + 1)],
                     [("m2", s * d)],
-                    cost=0.1,
+                    cost=0.04,
                     sends=[("az", dy, s, d)],
                 )
-        task(("az", dy, 0), [("az", dy, s, 1) for s in SIGNS], [("m2", 0)], cost=0.15)
-    task(("ay", 2), after=[("az", 2, 0)], cost=0.1, sends=[("ay", s, 2) for s in SIGNS])
+        task(("az", dy, 0), [("az", dy, s, 1) for s in SIGNS], [("m2", 0)], cost=0.04)
+    task(("ay", 2), after=[("az", 2, 0)], cost=0.04, sends=[("ay", s, 2) for s in SIGNS])
     for s in SIGNS:
-        task(("ay", s, 1), [("ay", s, 2)], [("az", s, 0)], cost=0.1, sends=[("ay", s, 1)])
+        task(("ay", s, 1), [("ay", s, 2)], [("az", s, 0)], cost=0.04, sends=[("ay", s, 1)])
     task(
-        ("xa",), [("ay", s, 1) for s in SIGNS], [("az", 0, 0)], cost=0.15, sends=[("xa",)]
+        ("xa",), [("ay", s, 1) for s in SIGNS], [("az", 0, 0)], cost=0.04, sends=[("xa",)]
     )
     for dz in range(-3, 5):
-        task(("by", dz, 2), after=[("m2", dz)], cost=0.1, sends=[("by", dz, s, 2) for s in SIGNS])
+        task(("by", dz, 2), after=[("m2", dz)], cost=0.04, sends=[("by", dz, s, 2) for s in SIGNS])
         for s in SIGNS:
             task(
                 ("by", dz, s, 1),
                 [("by", dz, s, 2)],
                 [("m2", dz)],
-                cost=0.15,
+                cost=0.04,
                 sends=[("by", dz, s, 1)],
             )
-        task(("by", dz, 0), [("by", dz, s, 1) for s in SIGNS], [("m2", dz)], cost=0.2)
-    task(("bz", 4), after=[("by", 4, 0)], cost=0.1, sends=[("bz", s, 4) for s in SIGNS])
+        task(("by", dz, 0), [("by", dz, s, 1) for s in SIGNS], [("m2", dz)], cost=0.06)
+    task(("bz", 4), after=[("by", 4, 0)], cost=0.04, sends=[("bz", s, 4) for s in SIGNS])
     for s in SIGNS:
         for d in (3, 2, 1):
             task(
                 ("bz", s, d),
                 [("bz", s, d + 1)],
                 [("by", s * d, 0)],
-                cost=0.15,
+                cost=0.04,
                 sends=[("bz", s, d)],
             )
-    task(("xb",), [("bz", s, 1) for s in SIGNS], [("by", 0, 0)], cost=0.2, sends=[("xb",)])
+    task(("xb",), [("bz", s, 1) for s in SIGNS], [("by", 0, 0)], cost=0.06, sends=[("xb",)])
+    for n, dz in enumerate(ORDER):
+        task(("cx", dz), after=[("m2", dz)], cost=0.04, sends=[("cx", dz)])
+        task(("cs", dz), [("cx", dz)], [("m2", dz)], cost=0.04)
+    for g in (0, 1):
+        done = [("cs", dz) for dz in GROUPS[g]]
+        task(("cy", g, 2), after=done, cost=0.04, sends=[("cy", g, s, 2) for s in SIGNS])
+        for s in SIGNS:
+            task(("cy", g, s, 1), [("cy", g, s, 2)], done, cost=0.04, sends=[("cy", g, s, 1)])
+        task(("cy", g, 0), [("cy", g, s, 1) for s in SIGNS], done, cost=0.04)
+    task(("cz", 4), after=[("cy", 0, 0)], cost=0.03, sends=[("cz", s, 4) for s in SIGNS])
+    for s in SIGNS:
+        for d in (3, 2, 1):
+            task(
+                ("cz", s, d),
+                [("cz", s, d + 1)],
+                [("cy", 0 if s * d in GROUPS[0] else 1, 0)],
+                cost=0.03,
+                sends=[("cz", s, d)],
+            )
+    task(("xc",), [("cz", s, 1) for s in SIGNS], [("cy", 1, 0)], cost=0.03, sends=[("xc",)])
     for k in range(4):
         needs, after = [], [("m2", ORDER[-1])]
         if k == 0:
@@ -233,7 +277,7 @@
         else:
             after += [("p8", k - 1)]
         task(("p8", k), needs, after, cost=1.3)
-    task(("g1",), after=[("p8", 3)], cost=0.1, sends=[("g1z", k) for k in range(1, NZ)])
+    task(("g1",), after=[("p8", 3)], cost=0.1, sends=[("g1z", k) for k in FAR])
     task(
         ("g2",), [("g1z", k) for k in range(1, NZ)], [("g1",)], 0.1, [("g1y", k) for k in range(1, NY)]
     )
@@ -245,6 +289,7 @@
 
 PLANES = ((0,), (1, -1), (2, -2), (3, -3), (4,))
 ORDER = (4, 3, -3, 2, -2, 1, -1, 0)
+GROUPS = (ORDER[:4], ORDER[4:])
 
 
 def schedule(tasks):
@@ -273,18 +318,19 @@
     left = dict(tasks)
     while left:
         ready, soonest = [], None
-        for name, (needs, after, _, _) in left.items():
+        for name, (needs, after, cost, sends) in left.items():
             if any(a not in done for a in after) or any(m not in arrives for m in needs):
                 continue
             at = max([arrives[m] for m in needs], default=0.0)
             if at <= now:
-                ready.append((-rank(name), at, name))
+                heavy = cost >= 0.3 and not sends
+                ready.append((heavy, -rank(name), at, name))
             else:
                 soonest = at if soonest is None else min(soonest, at)
         if not ready:
             now = soonest
             continue
-        name = min(ready, key=lambda r: (r[0], r[1]))[2]
+        name = min(ready, key=lambda r: r[:3])[3]
         _, _, cost, sends = left.pop(name)
         now += cost
         done[name] = now
@@ -305,9 +351,10 @@
 def kernel(
     order, tasks, index,
     x_hbm, hid_ref, res_ref, basis_ref,
-    new_ref, hess_ref, proj_ref,
-    xv, q, p, send_a, send_b, recv_a, recv_b, acc, img, r, v16, ht, hs, cur,
-    early, late, gz, gy, gx, square, load_sem, send_sem, recv_sem,
+    own_ref, first_ref, second_ref,
+    xv, q, qc, xc, select, p, send_a, send_b, recv_a, recv_b,
+    send_cx, recv_cx, send_cy, recv_cy, send_cz, recv_cz, acc, img, r, v16, ht, hs, cur,
+    early, gz, gy, gx, hz, hw, load_sem, send_sem, recv_sem,
 ):
     dp, fs = lax.axis_index("dp"), lax.axis_index("fsdp")
     z, y, xh = fs // 8, lax.rem(fs // 2, 4), lax.rem(fs, 2)
@@ -334,14 +381,34 @@
         ca = 1 - core if k & 1 else core
         return (la * 2 + ca, fsdp(z, y, xa))
 
-    partners = [along_z(d) for d in range(1, NZ)] + [along_y(d) for d in range(1, NY)]
-    partners += [along_x(k) for k in range(1, 8)]
+    def along_w(k):
+        bits = k & 7
+        xa = 1 - xh if bits & 4 else xh
+        la = 1 - xl if bits & 2 else xl
+        ca = 1 - core if bits & 1 else core
+        return (la * 2 + ca, fsdp(z, yi[k // 8], xa))
+
+    partners = [along_z(d) for d in FAR] + [along_w(k) for k in WIDE]
 
     loading = pltpu.make_async_copy(x_hbm, xv, load_sem)
     loading.start()
     barrier = pltpu.get_barrier_semaphore()
     for device in partners:
         pl.semaphore_signal(barrier, inc=1, device_id=device, device_id_type=MESH)
+    q[:, :, other, pl.ds(ROWS_A + ROWS_B, ROWS_C)] = jnp.zeros((NZ, NY, ROWS_C, WID), BF)
+    narrow = basis_ref[K - 1].astype(BF)
+    q[z, y, xh] = narrow
+    v16[K - 1, xh] = narrow
+    r[z, y] = res_ref[...]
+    for n in range(K - 1):
+        v16[n, xh] = basis_ref[n].astype(BF)
+    turned = []
+    for which in (0, 1):
+        pieces = [hid_ref[:, (2 * n + which) * 64 : (2 * n + which + 1) * 64] for n in range(8)]
+        turned.append(jnp.concatenate(pieces, axis=1))
+    hs[0] = turned[0]
+    hs[1] = turned[1]
+    ht[xl, core, xh] = hs[xh]
 
     def q_part(rows, part, oz, oy):
         at = q.at[zi[oz], yi[oy]]
@@ -349,6 +416,10 @@
         return at.at[which, rows]
 
     a_rows, b_rows = pl.ds(0, ROWS_A), pl.ds(ROWS_A, ROWS_B)
+    c_rows = pl.ds(ROWS_A + ROWS_B, ROWS_C)
+
+    def lane_half(sign):
+        return pl.ds(half_of(sign) * (WID // 2), WID // 2)
 
     def slot_a(msg):
         if msg[0] == "az":
@@ -376,8 +447,37 @@
     def place(msg):
         kind = msg[0]
         if kind == "qx":
-            here = q.at[z, y, xh]
-            return here, here, q.at[z, y, other], along_x(4)
+            rows = pl.ds(0, ROWS_A + ROWS_B)
+            here = q.at[z, y, xh, rows]
+            return here, here, q.at[z, y, other, rows], along_x(4)
+        if kind == "Cz":
+            _, s, h = msg
+            lanes = lane_half(s) if h == 4 else slice(None)
+            here = q.at[zi[wrap(-s * (h - 1), NZ)], y, xh, c_rows, lanes]
+            return here, here, q.at[zi[wrap(-s * h, NZ)], y, xh, c_rows, lanes], along_z(s)
+        if kind == "Cy":
+            _, s, h = msg
+            lanes = lane_half(s) if h == 2 else slice(None)
+            here = q.at[:, yi[wrap(-s * (h - 1), NY)], xh, c_rows, lanes]
+            return here, here, q.at[:, yi[wrap(-s * h, NY)], xh, c_rows, lanes], along_y(s)
+        if kind == "Cx":
+            lands = qc.at[:, yi[msg[1]]]
+            return q.at[:, yi[msg[1]], xh, c_rows], lands, lands, along_x(4)
+        if kind == "cx":
+            n = ORDER.index(msg[1])
+            return send_cx.at[n], recv_cx.at[n], recv_cx.at[n], along_x(4)
+        if kind == "cy":
+            _, g, s, d = msg
+            n, lanes = (2, lane_half(s)) if d == 2 else (half_of(s), slice(None))
+            target = recv_cy.at[g, n, :, :, lanes]
+            return send_cy.at[g, n, :, :, lanes], target, target, along_y(s)
+        if kind == "cz":
+            _, s, d = msg
+            n, lanes = (6, lane_half(s)) if d == 4 else ((d - 1) * 2 + half_of(s), slice(None))
+            target = recv_cz.at[n, :, lanes]
+            return send_cz.at[n, :, lanes], target, target, along_z(s)
+        if kind == "xc":
+            return send_cz.at[7], recv_cz.at[7], recv_cz.at[7], along_x(4)
         if kind in ("Ay", "Az", "Bz", "By"):
             rows = a_rows if kind[0] == "A" else b_rows
             if kind in ("Ay", "Bz"):
@@ -399,24 +499,24 @@
         if kind in ("Ry", "RZ", "Rz", "RY"):
             _, s, h = msg
             last = h == (NY if kind[1] in "yY" else NZ) // 2
-            low = 0 if kind in ("Ry", "RZ") else 32
-            rows = pl.ds(low + 16 * half_of(s), 16) if last else pl.ds(low, 32)
+            rows = pl.ds(0, 16) if kind in ("Ry", "RZ") else pl.ds(16, 48)
+            lanes = lane_half(s) if last else slice(None)
             n = NY if kind[1] in "yY" else NZ
             a, b = wrap(-s * (h - 1), n), wrap(-s * h, n)
             if kind == "Ry":
-                here, there = r.at[z, yi[a], rows], r.at[z, yi[b], rows]
+                here, there = r.at[z, yi[a], rows, lanes], r.at[z, yi[b], rows, lanes]
             elif kind == "Rz":
-                here, there = r.at[zi[a], y, rows], r.at[zi[b], y, rows]
+                here, there = r.at[zi[a], y, rows, lanes], r.at[zi[b], y, rows, lanes]
             elif kind == "RZ":
-                here, there = r.at[zi[a], :, rows], r.at[zi[b], :, rows]
-            else:
-                here, there = r.at[:, yi[a], rows], r.at[:, yi[b], rows]
+                here, there = r.at[zi[a], :, rows, lanes], r.at[zi[b], :, rows, lanes]
+            else:
+                here, there = r.at[:, yi[a], rows, lanes], r.at[:, yi[b], rows, lanes]
             return here, here, there, along_y(s) if n == NY else along_z(s)
         if kind == "vx":
             here = v16.at[pl.ds(0, K - 1), xh]
             return here, here, v16.at[pl.ds(0, K - 1), other], along_x(4)
         if kind == "hx":
-            return hs, ht.at[xl, core, xh], ht.at[xl, core, other], along_x(4)
+            return hs.at[other], ht.at[xl, core, xh], ht.at[xl, core, other], along_x(4)
         if kind == "hl":
             here = ht.at[xl, core]
             return here, here, ht.at[1 - xl, core], along_x(2)
@@ -437,16 +537,26 @@
             return src, target, target, along_z(msg[2]) if kind == "az" else along_y(msg[2])
         if kind in ("ay", "bz"):
             return src, target, target, along_y(msg[1]) if kind == "ay" else along_z(msg[1])
-        lane, k = int(kind[1]) - 1, msg[1]
-        if kind[2] == "z":
-            return gz.at[lane, z], gz.at[lane, z], gz.at[lane, zi[-k + NZ if k > 3 else -k]], along_z(k)
-        if kind[2] == "y":
-            return gy.at[lane, y], gy.at[lane, y], gy.at[lane, yi[-k + NY if k > 1 else -k]], along_y(k)
-        mine = xh * 4 + xl * 2 + core
+        k = msg[1]
+        if kind == "g1z":
+            here = gz.at[z]
+            return here, here, gz.at[zi[-k + NZ if k > 3 else -k]], along_z(k)
+        if kind == "g1y":
+            here = gy.at[y]
+            return here, here, gy.at[yi[-k + NY if k > 1 else -k]], along_y(k)
+        if kind == "g2z":
+            here = hz.at[z, pl.ds(0, 2)]
+            return here, here, hz.at[zi[-k + NZ if k > 3 else -k], pl.ds(0, 2)], along_z(k)
         xa = 1 - xh if k & 4 else xh
         la = 1 - xl if k & 2 else xl
         ca = 1 - core if k & 1 else core
-        return gx.at[lane, mine], gx.at[lane, mine], gx.at[lane, xa * 4 + la * 2 + ca], along_x(k)
+        mine, theirs = xh * 4 + xl * 2 + core, xa * 4 + la * 2 + ca
+        if kind == "g1x":
+            return gx.at[mine], gx.at[mine], gx.at[theirs], along_x(k)
+        d = k // 8
+        here = hw.at[y * 8 + mine, pl.ds(0, 2)]
+        lands = hw.at[yi[-d + NY if d > 1 else -d] * 8 + theirs, pl.ds(0, 2)]
+        return here, here, lands, along_w(k)
 
     started = []
 
@@ -485,6 +595,18 @@
     def fold_b(where, msgs, out=None):
         fold(b_rows, recv_b, where, [slot_b(m) for m in msgs], out and (send_b, slot_b(out)[0]))
 
+    def fold_c(plane, row, arrived, out=None):
+        for h in (0, 1):
+            lanes = pl.ds(h * (WID // 2), WID // 2)
+            total = p[plane, row, xh, c_rows, lanes]
+            for ref, s in arrived:
+                if s is None or half_of(s) == h:
+                    total = total + ref[:, lanes].astype(F32)
+            if out is None:
+                p[plane, row, xh, c_rows, lanes] = total
+            else:
+                out[:, lanes] = total.astype(BF)
+
     def lanes_of(plane):
         return pl.ds(pl.multiple_of(plane * (NY * 2 * BLK), 128), NY * 2 * BLK)
 
@@ -495,36 +617,24 @@
         n = rows.shape[0] // (2 * BLK)
         return jnp.sum(mapped.reshape(n, 2 * BLK, 512) * hidden[None], axis=1)
 
-    def per_example(tokens, k):
+    def per_example(tokens):
         t = lax.broadcasted_iota(jnp.int32, (512, 128), 0)
         e = lax.broadcasted_iota(jnp.int32, (512, 128), 1)
-        owner = 32 * k + (t // 64) * 4 + 2 * xh + lax.rem(t, 64) // EX_TOK
-        marks = jnp.where(owner == e, 1.0, 0.0).astype(F32)
-        return jnp.dot(tokens, marks, precision=lax.Precision.HIGHEST, preferred_element_type=F32)
+        owner = (t // 64) * 4 + 2 * xh + lax.rem(t, 64) // EX_TOK
+        marks = jnp.where(owner == lax.rem(e, 32), 1.0, 0.0).astype(BF)
+        terms, rest = [], tokens
+        for _ in range(3):
+            terms.append(rest.astype(BF).astype(F32))
+            rest = rest - terms[-1]
+        sums = product(jnp.concatenate(terms, axis=0).astype(BF), marks, 1, 0)
+        return sums[0:8] + sums[8:16] + sums[16:24]
 
     def work(name):
         kind = name[0]
         if kind == "start":
-            narrow = basis_ref[K - 1].astype(BF)
-            q[z, y, xh] = narrow
-            v16[K - 1, xh] = narrow
-            r[z, y] = res_ref[...]
             pl.semaphore_wait(barrier, len(partners))
         elif kind == "vx":
-            for n in range(K - 1):
-                v16[n, xh] = basis_ref[n].astype(BF)
-            v16[K - 1, other] = q[z, y, other]
-        elif kind == "hx":
-            eye_a = lax.broadcasted_iota(jnp.int32, (BLK, BLK), 0)
-            eye_b = lax.broadcasted_iota(jnp.int32, (BLK, BLK), 1)
-            eye = jnp.where(eye_a == eye_b, 1.0, 0.0).astype(BF)
-
-            def turned(which):
-                rows = [hid_ref[pl.ds(pl.multiple_of((2 * n + which) * 64, 64), 64), :] for n in range(8)]
-                return product(eye, jnp.concatenate(rows, axis=0), 1, 1).astype(BF)
-
-            ht[xl, core, xh] = turned(xh)
-            hs[...] = turned(other)
+            pass
         elif kind == "gram":
             lane = lax.broadcasted_iota(jnp.int32, (8, 128), 1)
             table = jnp.zeros((8, 128), F32)
@@ -542,6 +652,19 @@
                 term = product(xv[:, lanes_of(zi[dz])], q[zi[dz]].reshape(NY * 2 * BLK, WID), 1, 0)
                 total = term if total is None else total + term
             acc[...] = total if name[1] == 0 else acc[...] + total
+        elif kind == "xs":
+            k = name[1]
+            if k == 0:
+                f = lax.broadcasted_iota(jnp.int32, (1280, 128), 0)
+                at = lax.broadcasted_iota(jnp.int32, (1280, 128), 1)
+                block = (f * 52429) >> 22
+                inside = f - block * BLK - (ROWS_A + ROWS_B)
+                hit = (inside >= 0) & ((block & 1) == other) & ((block >> 1) * ROWS_C + inside == at)
+                select[...] = jnp.where(hit, 1.0, 0.0).astype(BF)
+            columns = xv[:, 1280 * k : 1280 * (k + 1)]
+            xc[:, 128 * k : 128 * (k + 1)] = product(columns, select[...], 1, 0).astype(BF)
+        elif kind == "m1c":
+            acc[...] = acc[...] + product(xc[...], qc[...].reshape(NZ * NY * ROWS_C, WID), 1, 0)
         elif kind == "img":
             img[...] = acc[...].astype(BF)
         elif kind == "m2":
@@ -583,20 +706,53 @@
         elif kind == "xb":
             fold_b((z, y), [("bz", s, 1) for s in SIGNS])
             fold_b((z, y), [], ("xb",))
+        elif kind == "cx":
+            send_cx[ORDER.index(name[1])] = p[zi[name[1]], :, other, c_rows].astype(BF)
+        elif kind == "cs":
+            plane = zi[name[1]]
+            arrived = recv_cx[ORDER.index(name[1])].astype(F32)
+            p[plane, :, xh, c_rows] = p[plane, :, xh, c_rows] + arrived
+        elif kind == "cy":
+            g = name[1]
+            for j, dz in enumerate(GROUPS[g]):
+                if len(name) == 4:
+                    s = name[2]
+                    got = [(recv_cy.at[g, 2, j], s)]
+                    fold_c(zi[dz], yi[s], got, send_cy.at[g, half_of(s), j])
+                elif name[2] == 2:
+                    fold_c(zi[dz], yi[2], [], send_cy.at[g, 2, j])
+                else:
+                    fold_c(zi[dz], y, [(recv_cy.at[g, n, j], None) for n in (0, 1)])
+        elif kind == "cz":
+            if len(name) == 2:
+                fold_c(zi[4], y, [], send_cz.at[6])
+            else:
+                s, d = name[1:]
+                n = 6 if d == 3 else d * 2 + half_of(s)
+                got = [(recv_cz.at[n], s if d == 3 else None)]
+                fold_c(zi[s * d], y, got, send_cz.at[(d - 1) * 2 + half_of(s)])
+        elif kind == "xc":
+            fold_c(z, y, [(recv_cz.at[n], None) for n in (0, 1)])
+            fold_c(z, y, [], send_cz.at[7])
         elif kind == "p8":
             k = name[1]
-            early[0:8] = early[0:8] + per_example(per_token(v16[...].reshape(K * 2 * BLK, WID), k), k)
+            if k == 0:
+                v16[K - 1, other, pl.ds(0, ROWS_A + ROWS_B)] = q[z, y, other, pl.ds(0, ROWS_A + ROWS_B)]
+                v16[K - 1, other, c_rows] = qc[z, y]
+            sums = per_example(per_token(v16[...].reshape(K * 2 * BLK, WID), k))
+            lane = lax.broadcasted_iota(jnp.int32, (8, 128), 1)
+            early[0:8] = early[0:8] + jnp.where(lane // 32 == k, sums, 0.0)
         elif kind == "g1":
-            gz[0, z] = early[...]
+            gz[z] = early[...]
         elif kind == "g2":
-            gy[0, y] = ring_sum(gz, 0, NZ)
+            gy[y] = ring_sum(gz, NZ)
         elif kind == "g3":
-            gx[0, xh * 4 + xl * 2 + core] = ring_sum(gy, 0, NY)
-
-    def ring_sum(buf, lane, n):
-        total = buf[lane, 0]
+            gx[xh * 4 + xl * 2 + core] = ring_sum(gy, NY)
+
+    def ring_sum(buf, n, rows=16):
+        total = buf[0, 0:rows]
         for k in range(1, n):
-            total = total + buf[lane, k]
+            total = total + buf[k, 0:rows]
         return total
 
     for name in order:
@@ -610,7 +766,9 @@
 
     receive(("xa",))
     receive(("xb",))
-    mean = 1.0 / (FF * D)
+    receive(("xc",))
+    cur[xh, c_rows] = p[z, y, xh, c_rows] * (1.0 / TOKENS)
+    cur[other, c_rows] = recv_cz[7].astype(F32) * (1.0 / TOKENS)
     for k in (0, 1):
         cur[k, a_rows] = (p[z, y, k, a_rows] + recv_a[31, k].astype(F32)) * (1.0 / TOKENS)
         cur[k, b_rows] = (p[z, y, k, b_rows] + recv_b[31, k].astype(F32)) * (1.0 / TOKENS)
@@ -619,104 +777,120 @@
     rows.append(jnp.sum(mine * mine, axis=0, keepdims=True))
     rows.append(jnp.zeros((7, WID), F32))
     sums = jnp.sum(jnp.concatenate(rows, axis=0), axis=1, keepdims=True)
-    late[...] = jnp.broadcast_to(sums, (16, 128))
+    sub = lax.broadcasted_iota(jnp.int32, (16, 128), 0)
+    lane = lax.broadcasted_iota(jnp.int32, (16, 128), 1)
+    sums = jnp.sum(jnp.where(sub == lane, sums, 0.0), axis=0, keepdims=True)
     both = cur[...].reshape(2 * BLK, WID)
     high = both.astype(BF)
-    low = (both - high.astype(F32)).astype(BF)
-    pair = jnp.concatenate([high, low], axis=0)
-    shown = jnp.zeros((1, 128), F32)
-    for k in range(4):
-        tokens = per_token(pair, k)
-        tokens = tokens[0:1] + tokens[1:2]
-        shown = shown + per_example(jnp.broadcast_to(tokens, (8, 512)), k)[0:1]
-    late[9:10] = shown
-
-    gz[1, z] = late[...]
-    for k in range(1, NZ):
+    pair = jnp.concatenate([high, (both - high.astype(F32)).astype(BF)], axis=0)
+    tokens = [jnp.sum(per_token(pair, k), axis=0, keepdims=True) for k in range(4)]
+    tokens = jnp.concatenate(tokens + [jnp.zeros((4, 512), F32)], axis=0)
+    sub = lax.broadcasted_iota(jnp.int32, (8, 128), 0)
+    lane = lax.broadcasted_iota(jnp.int32, (8, 128), 1)
+    shown = jnp.where(lane // 32 == sub, per_example(tokens), 0.0)
+    shown = jnp.sum(shown, axis=0, keepdims=True)
+    hz[z, 0:1] = shown
+    hz[z, 1:2] = sums
+    for k in FAR:
         send(("g2z", k))
+    own_ref[...] = mine
     for k in range(1, 8):
         receive(("g1x", k))
-    first = ring_sum(gx, 0, 8)
+    first_ref[...] = ring_sum(gx, 8)
+    drain = list(started)
+    for copy in drain[:-40]:
+        copy.wait_send()
     for k in range(1, NZ):
         receive(("g2z", k))
-    gy[1, y] = ring_sum(gz, 1, NZ)
-    for k in range(1, NY):
-        send(("g2y", k))
-    for k in range(1, NY):
-        receive(("g2y", k))
-    gx[1, xh * 4 + xl * 2 + core] = ring_sum(gy, 1, NY)
-    for k in range(1, 8):
-        send(("g2x", k))
-    for k in range(1, 8):
-        receive(("g2x", k))
-    second = ring_sum(gx, 1, 8)
-
-    coeff = second[0:8] * mean
-    squared = second[8:9] * mean
+    hw[y * 8 + xh * 4 + xl * 2 + core, 0:2] = ring_sum(hz, NZ, 2)
+    for k in WIDE:
+        send(("g2w", k))
+    for copy in drain[-40:]:
+        copy.wait_send()
+    for k in WIDE:
+        receive(("g2w", k))
+    second_ref[0:2] = ring_sum(hw, 32, 2)
+    second_ref[2:8] = jnp.zeros((6, 128), F32)
+    for copy in started[len(drain):]:
+        copy.wait_send()
+
+
+def finish(own_ref, first_ref, second_ref, basis_ref, new_ref, hess_ref, proj_ref):
+    mean = 1.0 / (FF * D)
+    first, second = first_ref[...], second_ref[...]
     sub = lax.broadcasted_iota(jnp.int32, (8, 128), 0)
     lane = lax.broadcasted_iota(jnp.int32, (8, 128), 1)
-    row = jnp.sum(jnp.where(sub == lane, coeff, 0.0), axis=0, keepdims=True)
+    row = second[1:2] * mean
+    coeff = jnp.sum(jnp.where(sub == lane, row, 0.0), axis=1, keepdims=True)
+    squared = jnp.sum(jnp.where(lane[0:1] == K, row, 0.0), axis=1, keepdims=True)
+    row = jnp.where(lane[0:1] < K, row, 0.0)
     cross = jnp.sum(coeff * first[8:16], axis=0, keepdims=True) * row
     cross = jnp.sum(cross, axis=1, keepdims=True) * mean
-    twice = 2.0 * jnp.sum(coeff * coeff, axis=0, keepdims=True)
+    twice = 2.0 * jnp.sum(row * row, axis=1, keepdims=True)
     beta = jnp.sqrt(jnp.maximum(squared - twice + cross, squared * 1e-12))
     inverse = 1.0 / beta
-    lane1 = lax.broadcasted_iota(jnp.int32, (1, 128), 1)
-    hess_ref[...] = jnp.where(lane1 == K, beta, row)[:, 0 : K + 1]
-    left = mine
+    hess_ref[...] = jnp.where(lane[0:1] == K, beta, row)[:, 0 : K + 1]
+    left = own_ref[...]
     for n in range(K):
-        left = left - coeff[n : n + 1, 0:1] * basis_ref[n]
-    new_ref[0] = left * inverse[:, 0:1]
-    last = (second[9:10] - jnp.sum(coeff * first[0:8], axis=0, keepdims=True)) * inverse
+        left = left - coeff[n : n + 1] * basis_ref[n]
+    new_ref[0] = left * inverse
+    last = (second[0:1] - jnp.sum(coeff * first[0:8], axis=0, keepdims=True)) * inverse
     scale = (FF * D) ** (-0.5)
-    square[...] = jnp.zeros((128, 128), F32)
-    square[0:8] = first[0:8] * scale
-    square[8:9] = last * scale
-    square[...] = square[...].T
-    proj_ref[...] = square[pl.ds(pl.multiple_of(dp * 32, 32), 32), 0 : K + 1]
-    for copy in started:
-        copy.wait_send()
+    shown = jnp.concatenate([first[0:8], jnp.broadcast_to(last, (8, 128))], axis=0) * scale
+    dp = lax.axis_index("dp")
+    for n in range(4):
+        @pl.when(dp == n)
+        def _():
+            proj_ref[...] = shown[0 : K + 1, n * 32 : (n + 1) * 32]
 
 
 def local(train_hidden, index_hidden, index_resid, basis):
     tasks = build()
     order, _, _ = schedule(tasks)
     messages = [m for name in tasks for m in tasks[name][3]]
-    messages += [("g2z", k) for k in range(1, NZ)] + [("g2y", k) for k in range(1, NY)]
-    messages += [("g2x", k) for k in range(1, 8)]
+    messages += [("g2z", k) for k in FAR] + [("g2w", k) for k in WIDE]
     index = {m: n for n, m in enumerate(messages)}
     vmem = pltpu.VMEM
     whole = pl.BlockSpec(memory_space=pltpu.VMEM)
     call = pl.pallas_call(
         functools.partial(kernel, order, tasks, index),
         out_shape=(
-            jax.ShapeDtypeStruct((1, BLK, WID), F32),
-            jax.ShapeDtypeStruct((1, K + 1), F32),
-            jax.ShapeDtypeStruct((32, K + 1), F32),
+            jax.ShapeDtypeStruct((BLK, WID), F32),
+            jax.ShapeDtypeStruct((16, 128), F32),
+            jax.ShapeDtypeStruct((8, 128), F32),
         ),
         in_specs=[pl.BlockSpec(memory_space=pl.ANY), whole, whole, whole],
         out_specs=(whole, whole, whole),
         scratch_shapes=[
             vmem((1024, FF), BF),
             vmem((NZ, NY, 2, BLK, WID), BF),
+            vmem((NZ, NY, ROWS_C, WID), BF),
+            vmem((1024, NZ * NY * ROWS_C), BF),
+            vmem((1280, 128), BF),
             vmem((NZ, NY, 2, BLK, WID), F32),
             vmem((32, 2, ROWS_A, WID), BF),
             vmem((32, 2, ROWS_B, WID), BF),
             vmem((32, 2, ROWS_A, WID), BF),
             vmem((32, 2, ROWS_B, WID), BF),
+            vmem((NZ, NY, ROWS_C, WID), BF),
+            vmem((NZ, NY, ROWS_C, WID), BF),
+            vmem((2, 3, 4, ROWS_C, WID), BF),
+            vmem((2, 3, 4, ROWS_C, WID), BF),
+            vmem((8, ROWS_C, WID), BF),
+            vmem((8, ROWS_C, WID), BF),
             vmem((1024, WID), F32),
             vmem((1024, WID), BF),
             vmem((NZ, NY, 64, WID), BF),
             vmem((K, 2, BLK, WID), BF),
             vmem((2, 2, 2, BLK, WID), BF),
-            vmem((BLK, WID), BF),
+            vmem((2, BLK, WID), BF),
             vmem((2, BLK, WID), F32),
             vmem((16, 128), F32),
-            vmem((16, 128), F32),
-            vmem((2, NZ, 16, 128), F32),
-            vmem((2, NY, 16, 128), F32),
-            vmem((2, 8, 16, 128), F32),
-            vmem((128, 128), F32),
+            vmem((NZ, 16, 128), F32),
+            vmem((NY, 16, 128), F32),
+            vmem((8, 16, 128), F32),
+            vmem((NZ, 8, 128), F32),
+            vmem((32, 8, 128), F32),
             pltpu.SemaphoreType.DMA,
             pltpu.SemaphoreType.DMA((len(messages),)),
             pltpu.SemaphoreType.DMA((len(messages),)),
@@ -729,7 +903,19 @@
         ),
         name="arnoldi",
     )
-    return call(train_hidden, index_hidden, index_resid, basis)
+    own, first, second = call(train_hidden, index_hidden.T, index_resid, basis)
+    new, hess, proj = pl.pallas_call(
+        finish,
+        out_shape=(
+            jax.ShapeDtypeStruct((1, BLK, WID), F32),
+            jax.ShapeDtypeStruct((1, K + 1), F32),
+            jax.ShapeDtypeStruct((K + 1, 32), F32),
+        ),
+        in_specs=[whole] * 4,
+        out_specs=(whole, whole, whole),
+        name="finish",
+    )(own, first, second, basis)
+    return new, hess, proj.T
 
 
 def solution(mesh):

time: 125 us -> 115 us (0.920)
  local copies, waits for them, and re-layouts: 5.91 us -> 0 us
  Pallas kernels: 118 us -> 115 us
    unnamed x3 -> x0, local copies, waits for them, and re-layouts: 4.51 us -> none
    pallas_call x1 -> x2, Pallas kernels: 118 us -> 115 us  [the longest x1 112 us: local(): own, first, second = call(train_hidden, index_hidden.T, index_resid, basis)]
    pallas_call x1 -> x0, local copies, waits for them, and re-layouts: 1.39 us -> none  [local(): return call(train_hidden, index_hidden, index_resid, basis)]
where the time goes in v2:
time: 115 us
  Pallas kernels  115 us (100%)
    pallas_call x1, Pallas kernels, local(): own, first, second = call(train_hidden, index_hidden.T, index_resid, basis)  112 us
    pallas_call x1, Pallas kernels, local(): pl.pallas_call(finish, out_shape=(jax.ShapeDtypeStruct((1, BLK, WID), F32...  2.42 us

profile of v2, /device:TPU:1, one launch (start us, length us, event | category | flops | bytes accessed | tf_op | source)
XLA Modules:
  0.0 115.3 jit_solution(459612173256709080)
XLA Ops:
  0.6 112.2 %arnoldi.1 = (f32[80,512]{1,0:T(8,128)}, f32[16,128]{1,0:T(8,128)}, f32[8,128]{1,0:T(8,128)}) custom-call(bf16[1024,5120]{1,0:T(8,128)(2,1)} %x_hbm.1, bf16[80,1024]{1,0:T(8,128)(2,1)} %bitcast.2, bf16[64,512]{1,0:T(8,128)(2,1)} %res_ref.1, f32[8,80,512]{2,1,0:T(8,128)} %basis_ref.3), custom_call_target="tpu_custom_call" | custom-call | flops 14000000000 | bytes 13000000 | tf_op jit(solution)/shard_map/arnoldi/pallas_call | solution.py:906
  112.9 2.4 %finish.1 = (f32[1,80,512]{2,1,0:T(8,128)}, f32[1,9]{1,0:T(1,128)}, f32[9,32]{1,0:T(8,128)}) custom-call(f32[80,512]{1,0:T(8,128)} %get-tuple-element.9.own_ref, f32[16,128]{1,0:T(8,128)} %get-tuple-element.10.first_ref, f32[8,128]{1,0:T(8,128)} %get-tuple-element.11.second_ref, f32[8,80,512]{2,1,0:T(8,128)} %basis_ref.3), custom_call_target="tpu_custom_call" | custom-call | tf_op jit(solution)/shard_map/finish/pallas_call | solution.py:907

commit v3 on v2

--- a/solution.py
+++ b/solution.py
@@ -155,8 +155,13 @@
         sends=[("Cx", 0)] + [("Cy", s, 1) for s in SIGNS],
     )
     task(("Cy2",), [("Cy", s, 2) for s in SIGNS], [("Cy", s) for s in SIGNS], sends=[("Cx", 2)])
-    late = [("Az", dy, s, 3) for dy in (0, 1, -1, 2) for s in SIGNS]
-    late += [("By", dz, s) for dz in range(-3, 5) for s in SIGNS]
+    late = {
+        0: [],
+        1: [("Bz4",)],
+        2: [("Az", dy, s, 2) for dy in (0, 1, -1, 2) for s in SIGNS],
+        3: [("Az", dy, s, 3) for dy in (0, 1, -1, 2) for s in SIGNS]
+        + [("By", dz, s) for dz in range(-3, 5) for s in SIGNS],
+    }[LATE]
     for s in SIGNS:
         task(("Ry", s), [("Ry", s, 1)], sends=[("Ry", s, 2)])
         for h in (1, 2, 3):
@@ -175,13 +180,15 @@
         [("Rz", s, h) for s in SIGNS for h in (1, 2, 3)] + late,
         sends=[("RY", s, 1) for s in SIGNS],
     )
-    task(("vx",), after=[("qx",), ("Cy2",)], cost=0.1, sends=[("vx",)])
-    task(("hx",), after=[("vx",)], sends=[("hx",)])
-    task(("hl",), [("hx",)], [("hx",)], sends=[("hl",)])
+    task(("vx",), after=[("start",)], cost=0.25, sends=[("vx",)])
+    task(("hx",), after=[("vx",)], cost=0.25, sends=[("hx",)])
+    task(("hl",), [("hx",)], [("hx",), ("Cy2",)], sends=[("hl",)])
     task(("hc",), [("hl",)], [("hl",)], sends=[("hc",)])
-    task(("gram",), after=[("qx",)], cost=2.0)
+    task(("gram",), after=[("vx",)], cost=0.8)
     for g, planes in enumerate(PLANES):
         needs, after = [], [("m1", g - 1)] if g else [("load",), ("CY0",), ("Cy2",)]
+        if g == len(PLANES) - 1:
+            after.append(("m1c",))
         for dz in planes:
             for s in SIGNS:
                 needs.append(("By", dz, s, 2, "f"))
@@ -204,7 +211,7 @@
         [("CY0",), ("Cy2",), ("m1", 0), ("xs", 3)],
         cost=0.9,
     )
-    task(("img",), after=[("m1", len(PLANES) - 1), ("m1c",)], cost=0.5)
+    task(("img",), after=[("m1", len(PLANES) - 1)], cost=0.0)
     for n, dz in enumerate(ORDER):
         task(("m2", dz), after=[("img",)] + ([("m2", ORDER[n - 1])] if n else []), cost=0.95)
     for dy in (0, 1, -1, 2):
@@ -267,7 +274,7 @@
                 sends=[("cz", s, d)],
             )
     task(("xc",), [("cz", s, 1) for s in SIGNS], [("cy", 1, 0)], cost=0.03, sends=[("xc",)])
-    for k in range(4):
+    for k in range(8):
         needs, after = [], [("m2", ORDER[-1])]
         if k == 0:
             needs += [("RZ", s, 4) for s in SIGNS] + [("RY", s, 2) for s in SIGNS]
@@ -276,25 +283,21 @@
             after += [("RZ0",), ("RY0",), ("hc",), ("vx",), ("gram",)]
         else:
             after += [("p8", k - 1)]
-        task(("p8", k), needs, after, cost=1.3)
-    task(("g1",), after=[("p8", 3)], cost=0.1, sends=[("g1z", k) for k in FAR])
-    task(
-        ("g2",), [("g1z", k) for k in range(1, NZ)], [("g1",)], 0.1, [("g1y", k) for k in range(1, NY)]
-    )
-    task(
-        ("g3",), [("g1y", k) for k in range(1, NY)], [("g2",)], 0.1, [("g1x", k) for k in range(1, 8)]
-    )
+        task(("p8", k), needs, after, cost=0.65)
+    task(("g1",), after=[("p8", 7)], cost=0.1, sends=[("g1z", k) for k in FAR])
     return tasks
 
 
 PLANES = ((0,), (1, -1), (2, -2), (3, -3), (4,))
 ORDER = (4, 3, -3, 2, -2, 1, -1, 0)
+LATE, RATE, DELAY, CLS = 1, 46.0, 1.4, True
+SLACK = {"Ry": 1.0, "Rz": 1.0, "RZ": 1.5, "RY": 1.5, "vx": 2.0, "hx": 2.0, "hl": 2.0, "hc": 2.0}
 GROUPS = (ORDER[:4], ORDER[4:])
 
 
 def schedule(tasks):
-    rate = {"z": 46.0, "y": 46.0, "x": 45.0, "c": 400.0}
-    delay = {"z": 1.5, "y": 1.5, "x": 2.0, "c": 0.8}
+    rate = {"z": RATE, "y": RATE, "x": RATE - 1, "c": 400.0}
+    delay = {"z": DELAY, "y": DELAY, "x": DELAY + 0.5, "c": 0.8}
     waits = {}
     followers = {name: [] for name in tasks}
     for name, (needs, after, _, _) in tasks.items():
@@ -323,7 +326,7 @@
                 continue
             at = max([arrives[m] for m in needs], default=0.0)
             if at <= now:
-                heavy = cost >= 0.3 and not sends
+                heavy = CLS and cost >= 0.3 and not sends
                 ready.append((heavy, -rank(name), at, name))
             else:
                 soonest = at if soonest is None else min(soonest, at)
@@ -340,7 +343,7 @@
             axis = link[0]
             begin = max(now, free.get(link, 0.0))
             free[link] = begin + kilobytes(msg) / rate.get(axis, 40.0)
-            arrives[msg] = free[link] + delay.get(axis, 3.0)
+            arrives[msg] = free[link] + delay.get(axis, 3.0) + SLACK.get(msg[0], 0.0)
     return order, done, arrives
 
 
@@ -350,11 +353,11 @@
 
 def kernel(
     order, tasks, index,
-    x_hbm, hid_ref, res_ref, basis_ref,
+    x_hbm, hid_hbm, res_hbm, basis_hbm,
     own_ref, first_ref, second_ref,
     xv, q, qc, xc, select, p, send_a, send_b, recv_a, recv_b,
     send_cx, recv_cx, send_cy, recv_cy, send_cz, recv_cz, acc, img, r, v16, ht, hs, cur,
-    early, gz, gy, gx, hz, hw, load_sem, send_sem, recv_sem,
+    early, tokens8, basis_ref, hid_ref, res_ref, gz, gy, gx, hz, hw, load_sem, send_sem, recv_sem,
 ):
     dp, fs = lax.axis_index("dp"), lax.axis_index("fsdp")
     z, y, xh = fs // 8, lax.rem(fs // 2, 4), lax.rem(fs, 2)
@@ -390,25 +393,27 @@
 
     partners = [along_z(d) for d in FAR] + [along_w(k) for k in WIDE]
 
-    loading = pltpu.make_async_copy(x_hbm, xv, load_sem)
-    loading.start()
     barrier = pltpu.get_barrier_semaphore()
+    loads = [
+        pltpu.make_async_copy(basis_hbm.at[K - 1], basis_ref.at[K - 1], load_sem.at[0]),
+        pltpu.make_async_copy(res_hbm, res_ref, load_sem.at[1]),
+        pltpu.make_async_copy(hid_hbm, hid_ref, load_sem.at[2]),
+        pltpu.make_async_copy(
+            basis_hbm.at[pl.ds(0, K - 1)], basis_ref.at[pl.ds(0, K - 1)], load_sem.at[3]
+        ),
+        pltpu.make_async_copy(x_hbm, xv, load_sem.at[4]),
+    ]
+    for load in loads:
+        load.start()
     for device in partners:
         pl.semaphore_signal(barrier, inc=1, device_id=device, device_id_type=MESH)
+    loads[0].wait()
+    loads[1].wait()
     q[:, :, other, pl.ds(ROWS_A + ROWS_B, ROWS_C)] = jnp.zeros((NZ, NY, ROWS_C, WID), BF)
     narrow = basis_ref[K - 1].astype(BF)
     q[z, y, xh] = narrow
     v16[K - 1, xh] = narrow
     r[z, y] = res_ref[...]
-    for n in range(K - 1):
-        v16[n, xh] = basis_ref[n].astype(BF)
-    turned = []
-    for which in (0, 1):
-        pieces = [hid_ref[:, (2 * n + which) * 64 : (2 * n + which + 1) * 64] for n in range(8)]
-        turned.append(jnp.concatenate(pieces, axis=1))
-    hs[0] = turned[0]
-    hs[1] = turned[1]
-    ht[xl, core, xh] = hs[xh]
 
     def q_part(rows, part, oz, oy):
         at = q.at[zi[oz], yi[oy]]
@@ -610,12 +615,16 @@
     def lanes_of(plane):
         return pl.ds(pl.multiple_of(plane * (NY * 2 * BLK), 128), NY * 2 * BLK)
 
-    def per_token(rows, k):
-        errors = r[2 * k : 2 * k + 2].reshape(512, WID)
-        hidden = ht[k // 2, k % 2].reshape(2 * BLK, 512).astype(F32)
-        mapped = product(rows, errors, 1, 1)
+    def per_token(rows, k, part=None):
+        if part is None:
+            many, errors, hidden = 512, r[2 * k : 2 * k + 2], ht[k // 2, k % 2]
+        else:
+            many, errors = 256, r[2 * k + part]
+            hidden = ht[k // 2, k % 2, :, :, 256 * part : 256 * (part + 1)]
+        mapped = product(rows, errors.reshape(many, WID), 1, 1)
         n = rows.shape[0] // (2 * BLK)
-        return jnp.sum(mapped.reshape(n, 2 * BLK, 512) * hidden[None], axis=1)
+        hidden = hidden.reshape(2 * BLK, many).astype(F32)
+        return jnp.sum(mapped.reshape(n, 2 * BLK, many) * hidden[None], axis=1)
 
     def per_example(tokens):
         t = lax.broadcasted_iota(jnp.int32, (512, 128), 0)
@@ -634,7 +643,16 @@
         if kind == "start":
             pl.semaphore_wait(barrier, len(partners))
         elif kind == "vx":
-            pass
+            loads[3].wait()
+            for n in range(K - 1):
+                v16[n, xh] = basis_ref[n].astype(BF)
+        elif kind == "hx":
+            loads[2].wait()
+            for which in (0, 1):
+                cuts = [(2 * n + which) * 64 for n in range(8)]
+                pieces = [hid_ref[:, at : at + 64] for at in cuts]
+                hs[which] = jnp.concatenate(pieces, axis=1)
+            ht[xl, core, xh] = hs[xh]
         elif kind == "gram":
             lane = lax.broadcasted_iota(jnp.int32, (8, 128), 1)
             table = jnp.zeros((8, 128), F32)
@@ -645,13 +663,16 @@
             early[8:16] = table
             early[0:8] = jnp.zeros((8, 128), F32)
         elif kind == "load":
-            loading.wait()
+            loads[4].wait()
         elif kind == "m1":
             total = None
             for dz in PLANES[name[1]]:
                 term = product(xv[:, lanes_of(zi[dz])], q[zi[dz]].reshape(NY * 2 * BLK, WID), 1, 0)
                 total = term if total is None else total + term
-            acc[...] = total if name[1] == 0 else acc[...] + total
+            if name[1] == len(PLANES) - 1:
+                img[...] = (acc[...] + total).astype(BF)
+            else:
+                acc[...] = total if name[1] == 0 else acc[...] + total
         elif kind == "xs":
             k = name[1]
             if k == 0:
@@ -666,7 +687,7 @@
         elif kind == "m1c":
             acc[...] = acc[...] + product(xc[...], qc[...].reshape(NZ * NY * ROWS_C, WID), 1, 0)
         elif kind == "img":
-            img[...] = acc[...].astype(BF)
+            pass
         elif kind == "m2":
             plane = zi[name[1]]
             p[plane] = product(xv[:, lanes_of(plane)], img[...], 0, 0).reshape(NY, 2, BLK, WID)
@@ -739,15 +760,14 @@
             if k == 0:
                 v16[K - 1, other, pl.ds(0, ROWS_A + ROWS_B)] = q[z, y, other, pl.ds(0, ROWS_A + ROWS_B)]
                 v16[K - 1, other, c_rows] = qc[z, y]
-            sums = per_example(per_token(v16[...].reshape(K * 2 * BLK, WID), k))
-            lane = lax.broadcasted_iota(jnp.int32, (8, 128), 1)
-            early[0:8] = early[0:8] + jnp.where(lane // 32 == k, sums, 0.0)
+            half = pl.ds(256 * (k % 2), 256)
+            tokens8[:, half] = per_token(v16[...].reshape(K * 2 * BLK, WID), k // 2, k % 2)
+            if k % 2:
+                sums = per_example(tokens8[...])
+                lane = lax.broadcasted_iota(jnp.int32, (8, 128), 1)
+                early[0:8] = early[0:8] + jnp.where(lane // 32 == k // 2, sums, 0.0)
         elif kind == "g1":
             gz[z] = early[...]
-        elif kind == "g2":
-            gy[y] = ring_sum(gz, NZ)
-        elif kind == "g3":
-            gx[xh * 4 + xl * 2 + core] = ring_sum(gy, NY)
 
     def ring_sum(buf, n, rows=16):
         total = buf[0, 0:rows]
@@ -794,9 +814,11 @@
     for k in FAR:
         send(("g2z", k))
     own_ref[...] = mine
-    for k in range(1, 8):
-        receive(("g1x", k))
-    first_ref[...] = ring_sum(gx, 8)
+    for k in FAR:
+        receive(("g1z", k))
+    gy[y] = ring_sum(gz, NZ)
+    for k in range(1, NY):
+        send(("g1y", k))
     drain = list(started)
     for copy in drain[:-40]:
         copy.wait_send()
@@ -807,6 +829,14 @@
         send(("g2w", k))
     for copy in drain[-40:]:
         copy.wait_send()
+    for k in range(1, NY):
+        receive(("g1y", k))
+    gx[xh * 4 + xl * 2 + core] = ring_sum(gy, NY)
+    for k in range(1, 8):
+        send(("g1x", k))
+    for k in range(1, 8):
+        receive(("g1x", k))
+    first_ref[...] = ring_sum(gx, 8)
     for k in WIDE:
         receive(("g2w", k))
     second_ref[0:2] = ring_sum(hw, 32, 2)
@@ -848,6 +878,7 @@
     tasks = build()
     order, _, _ = schedule(tasks)
     messages = [m for name in tasks for m in tasks[name][3]]
+    messages += [("g1y", k) for k in range(1, NY)] + [("g1x", k) for k in range(1, 8)]
     messages += [("g2z", k) for k in FAR] + [("g2w", k) for k in WIDE]
     index = {m: n for n, m in enumerate(messages)}
     vmem = pltpu.VMEM
@@ -859,7 +890,7 @@
             jax.ShapeDtypeStruct((16, 128), F32),
             jax.ShapeDtypeStruct((8, 128), F32),
         ),
-        in_specs=[pl.BlockSpec(memory_space=pl.ANY), whole, whole, whole],
+        in_specs=[pl.BlockSpec(memory_space=pl.ANY)] * 4,
         out_specs=(whole, whole, whole),
         scratch_shapes=[
             vmem((1024, FF), BF),
@@ -886,12 +917,16 @@
             vmem((2, BLK, WID), BF),
             vmem((2, BLK, WID), F32),
             vmem((16, 128), F32),
+            vmem((8, 512), F32),
+            vmem((K, BLK, WID), F32),
+            vmem((BLK, 1024), BF),
+            vmem((64, WID), BF),
             vmem((NZ, 16, 128), F32),
             vmem((NY, 16, 128), F32),
             vmem((8, 16, 128), F32),
             vmem((NZ, 8, 128), F32),
             vmem((32, 8, 128), F32),
-            pltpu.SemaphoreType.DMA,
+            pltpu.SemaphoreType.DMA((5,)),
             pltpu.SemaphoreType.DMA((len(messages),)),
             pltpu.SemaphoreType.DMA((len(messages),)),
         ],

time: 115 us -> 112 us (0.974)
  Pallas kernels: 115 us -> 111 us
    pallas_call x1, Pallas kernels: 112 us -> 109 us  [local(): own, first, second = call(train_hidden, index_hidden.T, index_resid, basis)]
where the time goes in v3:
time: 112 us
  Pallas kernels  111 us (99%)
    pallas_call x1, Pallas kernels, local(): own, first, second = call(train_hidden, index_hidden.T, index_resid, basis)  109 us
    pallas_call x1, Pallas kernels, local(): pl.pallas_call(finish, out_shape=(jax.ShapeDtypeStruct((1, BLK, WID), F32...  2.42 us

profile of v3, /device:TPU:1, one launch (start us, length us, event | category | flops | bytes accessed | tf_op | source)
XLA Modules:
  0.0 112.0 jit_solution(1093025081794533057)
XLA Ops:
  0.6 108.9 %arnoldi.1 = (f32[80,512]{1,0:T(8,128)}, f32[16,128]{1,0:T(8,128)}, f32[8,128]{1,0:T(8,128)}) custom-call(bf16[1024,5120]{1,0:T(8,128)(2,1)} %x_hbm.1, bf16[80,1024]{1,0:T(8,128)(2,1)} %bitcast.2, bf16[64,512]{1,0:T(8,128)(2,1)} %res_hbm.1, f32[8,80,512]{2,1,0:T(8,128)} %basis_ref.1), custom_call_target="tpu_custom_call" | custom-call | flops 14000000000 | bytes 13000000 | tf_op jit(solution)/shard_map/arnoldi/pallas_call | solution.py:941
  109.6 2.4 %finish.1 = (f32[1,80,512]{2,1,0:T(8,128)}, f32[1,9]{1,0:T(1,128)}, f32[9,32]{1,0:T(8,128)}) custom-call(f32[80,512]{1,0:T(8,128)} %get-tuple-element.9.own_ref, f32[16,128]{1,0:T(8,128)} %get-tuple-element.10.first_ref, f32[8,128]{1,0:T(8,128)} %get-tuple-element.11.second_ref, f32[8,80,512]{2,1,0:T(8,128)} %basis_ref.1), custom_call_target="tpu_custom_call" | custom-call | tf_op jit(solution)/shard_map/finish/pallas_call | solution.py:942

commit v4 on v3

--- a/solution.py
+++ b/solution.py
@@ -47,7 +47,9 @@
         return ("z", msg[2])
     if kind in ("Ay", "ay", "Ry", "RY", "Cy"):
         return ("y", msg[1])
-    if kind in ("Bz", "bz", "Rz", "RZ", "Cz", "cz"):
+    if kind == "cz":
+        return ("z", 1 if msg[1] < 4 else -1)
+    if kind in ("Bz", "bz", "Rz", "RZ", "Cz"):
         return ("z", msg[1])
     if kind in ("By", "by", "cy"):
         return ("y", msg[2])
@@ -79,7 +81,7 @@
         full = {"Ry": 16, "Rz": 48, "RZ": 64, "RY": 384, "Cz": ROWS_C, "Cy": 8 * ROWS_C}[kind]
         return full / 2 if msg[2] == (4 if kind[1] in "zZ" else 2) else full
     if kind == "cz":
-        return ROWS_C / 2 if msg[2] == 4 else ROWS_C
+        return 2 * ROWS_C
     if kind == "cy":
         return 2 * ROWS_C if msg[3] == 2 else 4 * ROWS_C
     if kind in ("Cx", "cx"):
@@ -263,17 +265,10 @@
         for s in SIGNS:
             task(("cy", g, s, 1), [("cy", g, s, 2)], done, cost=0.04, sends=[("cy", g, s, 1)])
         task(("cy", g, 0), [("cy", g, s, 1) for s in SIGNS], done, cost=0.04)
-    task(("cz", 4), after=[("cy", 0, 0)], cost=0.03, sends=[("cz", s, 4) for s in SIGNS])
-    for s in SIGNS:
-        for d in (3, 2, 1):
-            task(
-                ("cz", s, d),
-                [("cz", s, d + 1)],
-                [("cy", 0 if s * d in GROUPS[0] else 1, 0)],
-                cost=0.03,
-                sends=[("cz", s, d)],
-            )
-    task(("xc",), [("cz", s, 1) for s in SIGNS], [("cy", 1, 0)], cost=0.03, sends=[("xc",)])
+    for g in (0, 1):
+        sends = [("cz", dz % NZ) for dz in GROUPS[g] if dz]
+        task(("cz", g), after=[("cy", g, 0)], cost=0.05, sends=sends)
+    task(("xc",), [("cz", k) for k in FAR], [("cy", 1, 0)], cost=0.05, sends=[("xc",)])
     for k in range(8):
         needs, after = [], [("m2", ORDER[-1])]
         if k == 0:
@@ -290,7 +285,7 @@
 
 PLANES = ((0,), (1, -1), (2, -2), (3, -3), (4,))
 ORDER = (4, 3, -3, 2, -2, 1, -1, 0)
-LATE, RATE, DELAY, CLS = 1, 46.0, 1.4, True
+LATE, RATE, DELAY, CLS = 1, 46.0, 2.5, True
 SLACK = {"Ry": 1.0, "Rz": 1.0, "RZ": 1.5, "RY": 1.5, "vx": 2.0, "hx": 2.0, "hl": 2.0, "hc": 2.0}
 GROUPS = (ORDER[:4], ORDER[4:])
 
@@ -477,12 +472,10 @@
             target = recv_cy.at[g, n, :, :, lanes]
             return send_cy.at[g, n, :, :, lanes], target, target, along_y(s)
         if kind == "cz":
-            _, s, d = msg
-            n, lanes = (6, lane_half(s)) if d == 4 else ((d - 1) * 2 + half_of(s), slice(None))
-            target = recv_cz.at[n, :, lanes]
-            return send_cz.at[n, :, lanes], target, target, along_z(s)
+            n = msg[1]
+            return send_cz.at[n], recv_cz.at[n], recv_cz.at[n], along_z(n)
         if kind == "xc":
-            return send_cz.at[7], recv_cz.at[7], recv_cz.at[7], along_x(4)
+            return send_cz.at[0], recv_cz.at[0], recv_cz.at[0], along_x(4)
         if kind in ("Ay", "Az", "Bz", "By"):
             rows = a_rows if kind[0] == "A" else b_rows
             if kind in ("Ay", "Bz"):
@@ -745,16 +738,12 @@
                 else:
                     fold_c(zi[dz], y, [(recv_cy.at[g, n, j], None) for n in (0, 1)])
         elif kind == "cz":
-            if len(name) == 2:
-                fold_c(zi[4], y, [], send_cz.at[6])
-            else:
-                s, d = name[1:]
-                n = 6 if d == 3 else d * 2 + half_of(s)
-                got = [(recv_cz.at[n], s if d == 3 else None)]
-                fold_c(zi[s * d], y, got, send_cz.at[(d - 1) * 2 + half_of(s)])
+            for dz in GROUPS[name[1]]:
+                if dz:
+                    fold_c(zi[dz], y, [], send_cz.at[dz % NZ])
         elif kind == "xc":
-            fold_c(z, y, [(recv_cz.at[n], None) for n in (0, 1)])
-            fold_c(z, y, [], send_cz.at[7])
+            fold_c(z, y, [(recv_cz.at[n], None) for n in range(1, NZ)])
+            fold_c(z, y, [], send_cz.at[0])
         elif kind == "p8":
             k = name[1]
             if k == 0:
@@ -788,7 +777,7 @@
     receive(("xb",))
     receive(("xc",))
     cur[xh, c_rows] = p[z, y, xh, c_rows] * (1.0 / TOKENS)
-    cur[other, c_rows] = recv_cz[7].astype(F32) * (1.0 / TOKENS)
+    cur[other, c_rows] = recv_cz[0].astype(F32) * (1.0 / TOKENS)
     for k in (0, 1):
         cur[k, a_rows] = (p[z, y, k, a_rows] + recv_a[31, k].astype(F32)) * (1.0 / TOKENS)
         cur[k, b_rows] = (p[z, y, k, b_rows] + recv_b[31, k].astype(F32)) * (1.0 / TOKENS)

time: 112 us -> 108 us (0.964)
  Pallas kernels: 111 us -> 107 us
    pallas_call x1, Pallas kernels: 109 us -> 105 us  [local(): own, first, second = call(train_hidden, index_hidden.T, index_resid, basis)]
where the time goes in v4:
time: 108 us
  Pallas kernels  107 us (99%)
    pallas_call x1, Pallas kernels, local(): own, first, second = call(train_hidden, index_hidden.T, index_resid, basis)  105 us
    pallas_call x1, Pallas kernels, local(): pl.pallas_call(finish, out_shape=(jax.ShapeDtypeStruct((1, BLK, WID), F32...  2.42 us

profile of v4, /device:TPU:1, one launch (start us, length us, event | category | flops | bytes accessed | tf_op | source)
XLA Modules:
  0.0 108.0 jit_solution(2441637214488115352)
XLA Ops:
  0.6 104.9 %arnoldi.1 = (f32[80,512]{1,0:T(8,128)}, f32[16,128]{1,0:T(8,128)}, f32[8,128]{1,0:T(8,128)}) custom-call(bf16[1024,5120]{1,0:T(8,128)(2,1)} %x_hbm.1, bf16[80,1024]{1,0:T(8,128)(2,1)} %bitcast.2, bf16[64,512]{1,0:T(8,128)(2,1)} %res_hbm.1, f32[8,80,512]{2,1,0:T(8,128)} %basis_ref.1), custom_call_target="tpu_custom_call" | custom-call | flops 14000000000 | bytes 13000000 | tf_op jit(solution)/shard_map/arnoldi/pallas_call | solution.py:930
  105.5 2.4 %finish.1 = (f32[1,80,512]{2,1,0:T(8,128)}, f32[1,9]{1,0:T(1,128)}, f32[9,32]{1,0:T(8,128)}) custom-call(f32[80,512]{1,0:T(8,128)} %get-tuple-element.9.own_ref, f32[16,128]{1,0:T(8,128)} %get-tuple-element.10.first_ref, f32[8,128]{1,0:T(8,128)} %get-tuple-element.11.second_ref, f32[8,80,512]{2,1,0:T(8,128)} %basis_ref.1), custom_call_target="tpu_custom_call" | custom-call | tf_op jit(solution)/shard_map/finish/pallas_call | solution.py:931

commit v5 on v4

--- a/solution.py
+++ b/solution.py
@@ -285,8 +285,14 @@
 
 PLANES = ((0,), (1, -1), (2, -2), (3, -3), (4,))
 ORDER = (4, 3, -3, 2, -2, 1, -1, 0)
-LATE, RATE, DELAY, CLS = 1, 46.0, 2.5, True
-SLACK = {"Ry": 1.0, "Rz": 1.0, "RZ": 1.5, "RY": 1.5, "vx": 2.0, "hx": 2.0, "hl": 2.0, "hc": 2.0}
+BIAS = {
+    "By": 10, "Bz": 10, "RZ": -10, "RZ0": -20, "Ry": 10, "Rz": -10, "ay": 2, "az": -5,
+    "bz": -10, "cz": 5, "g1": -10, "hc": 2, "m1": -20, "m2": -5, "vx": -2, "xs": -20,
+}
+LATE, RATE, DELAY, CLS = 2, 46.0, 2.2, True
+SLACK = {
+    "Ry": 1, "Rz": 2, "RZ": 1.5, "RY": 3, "vx": 3, "hx": 1, "hl": 5, "hc": 0,
+}
 GROUPS = (ORDER[:4], ORDER[4:])
 
 
@@ -322,7 +328,7 @@
             at = max([arrives[m] for m in needs], default=0.0)
             if at <= now:
                 heavy = CLS and cost >= 0.3 and not sends
-                ready.append((heavy, -rank(name), at, name))
+                ready.append((heavy, -rank(name) - BIAS.get(name[0], 0.0), at, name))
             else:
                 soonest = at if soonest is None else min(soonest, at)
         if not ready:

time: 108 us -> 105 us (0.972)
  Pallas kernels: 107 us -> 104 us
    pallas_call x1, Pallas kernels: 105 us -> 102 us  [local(): own, first, second = call(train_hidden, index_hidden.T, index_resid, basis)]
where the time goes in v5:
time: 105 us
  Pallas kernels  104 us (99%)
    pallas_call x1, Pallas kernels, local(): own, first, second = call(train_hidden, index_hidden.T, index_resid, basis)  102 us
    pallas_call x1, Pallas kernels, local(): pl.pallas_call(finish, out_shape=(jax.ShapeDtypeStruct((1, BLK, WID), F32...  2.42 us

profile of v5, /device:TPU:1, one launch (start us, length us, event | category | flops | bytes accessed | tf_op | source)
XLA Modules:
  0.0 105.0 jit_solution(3620158245657226180)
XLA Ops:
  0.6 101.9 %arnoldi.1 = (f32[80,512]{1,0:T(8,128)}, f32[16,128]{1,0:T(8,128)}, f32[8,128]{1,0:T(8,128)}) custom-call(bf16[1024,5120]{1,0:T(8,128)(2,1)} %x_hbm.1, bf16[80,1024]{1,0:T(8,128)(2,1)} %bitcast.2, bf16[64,512]{1,0:T(8,128)(2,1)} %res_hbm.1, f32[8,80,512]{2,1,0:T(8,128)} %basis_ref.1), custom_call_target="tpu_custom_call" | custom-call | flops 14000000000 | bytes 13000000 | tf_op jit(solution)/shard_map/arnoldi/pallas_call | solution.py:936
  102.6 2.4 %finish.1 = (f32[1,80,512]{2,1,0:T(8,128)}, f32[1,9]{1,0:T(1,128)}, f32[9,32]{1,0:T(8,128)}) custom-call(f32[80,512]{1,0:T(8,128)} %get-tuple-element.9.own_ref, f32[16,128]{1,0:T(8,128)} %get-tuple-element.10.first_ref, f32[8,128]{1,0:T(8,128)} %get-tuple-element.11.second_ref, f32[8,80,512]{2,1,0:T(8,128)} %basis_ref.1), custom_call_target="tpu_custom_call" | custom-call | tf_op jit(solution)/shard_map/finish/pallas_call | solution.py:937

commit v6 on v5

--- a/solution.py
+++ b/solution.py
@@ -779,9 +779,19 @@
         for msg in sends:
             send(msg)
 
+    for k in FAR:
+        receive(("g1z", k))
+    gy[y] = ring_sum(gz, NZ)
+    for k in range(1, NY):
+        send(("g1y", k))
     receive(("xa",))
     receive(("xb",))
     receive(("xc",))
+    for k in range(1, NY):
+        receive(("g1y", k))
+    gx[xh * 4 + xl * 2 + core] = ring_sum(gy, NY)
+    for k in range(1, 8):
+        send(("g1x", k))
     cur[xh, c_rows] = p[z, y, xh, c_rows] * (1.0 / TOKENS)
     cur[other, c_rows] = recv_cz[0].astype(F32) * (1.0 / TOKENS)
     for k in (0, 1):
@@ -809,11 +819,6 @@
     for k in FAR:
         send(("g2z", k))
     own_ref[...] = mine
-    for k in FAR:
-        receive(("g1z", k))
-    gy[y] = ring_sum(gz, NZ)
-    for k in range(1, NY):
-        send(("g1y", k))
     drain = list(started)
     for copy in drain[:-40]:
         copy.wait_send()
@@ -824,11 +829,6 @@
         send(("g2w", k))
     for copy in drain[-40:]:
         copy.wait_send()
-    for k in range(1, NY):
-        receive(("g1y", k))
-    gx[xh * 4 + xl * 2 + core] = ring_sum(gy, NY)
-    for k in range(1, 8):
-        send(("g1x", k))
     for k in range(1, 8):
         receive(("g1x", k))
     first_ref[...] = ring_sum(gx, 8)

time: 105 us -> 105 us (level)
  no operation moved by 1% of the time
where the time goes in v6:
time: 105 us
  Pallas kernels  104 us (99%)
    pallas_call x1, Pallas kernels, local(): own, first, second = call(train_hidden, index_hidden.T, index_resid, basis)  102 us
    pallas_call x1, Pallas kernels, local(): pl.pallas_call(finish, out_shape=(jax.ShapeDtypeStruct((1, BLK, WID), F32...  2.42 us

profile of v6, /device:TPU:1, one launch (start us, length us, event | category | flops | bytes accessed | tf_op | source)
XLA Modules:
  0.0 105.1 jit_solution(4301524273717490062)
XLA Ops:
  0.6 102.1 %arnoldi.1 = (f32[80,512]{1,0:T(8,128)}, f32[16,128]{1,0:T(8,128)}, f32[8,128]{1,0:T(8,128)}) custom-call(bf16[1024,5120]{1,0:T(8,128)(2,1)} %x_hbm.1, bf16[80,1024]{1,0:T(8,128)(2,1)} %bitcast.2, bf16[64,512]{1,0:T(8,128)(2,1)} %res_hbm.1, f32[8,80,512]{2,1,0:T(8,128)} %basis_ref.1), custom_call_target="tpu_custom_call" | custom-call | flops 14000000000 | bytes 13000000 | tf_op jit(solution)/shard_map/arnoldi/pallas_call | solution.py:936
  102.7 2.4 %finish.1 = (f32[1,80,512]{2,1,0:T(8,128)}, f32[1,9]{1,0:T(1,128)}, f32[9,32]{1,0:T(8,128)}) custom-call(f32[80,512]{1,0:T(8,128)} %get-tuple-element.9.own_ref, f32[16,128]{1,0:T(8,128)} %get-tuple-element.10.first_ref, f32[8,128]{1,0:T(8,128)} %get-tuple-element.11.second_ref, f32[8,80,512]{2,1,0:T(8,128)} %basis_ref.1), custom_call_target="tpu_custom_call" | custom-call | tf_op jit(solution)/shard_map/finish/pallas_call | solution.py:937
